TPU v7x, 32 devices: a whole 2x2x4 slice. The times are simulated.
32 devices in a mesh: geom: 2 (over y), gx: 4 (over z), gy: 2 (over x), gz: 2 (over core).
Axes of the slice: x: 2, y: 2, z: 4, core: 2. Of those that a mesh axis runs over, the one named last changes fastest.
Arguments:
- features: bfloat16 [20480, 128], P(('geom', 'gx', 'gy', 'gz')), parts along dimension 0, may hold values from -6 to 6
- displacement: float32 [3, 983040], P(None, ('geom', 'gx', 'gy', 'gz')), parts along dimension 1, as said below
- neighbour: int32 [983040], P(('geom', 'gx', 'gy', 'gz')), parts along dimension 0, may hold values from 0 to 2687, as said below
- neighbour_count: int32 [20480], P(('geom', 'gx', 'gy', 'gz')), parts along dimension 0, may hold values from 12 to 48, as said below
- species: int32 [20480], P(('geom', 'gx', 'gy', 'gz')), parts along dimension 0, may hold values from 0 to 99
- exports_x: int32 [32, 2, 640], P(('geom', 'gx', 'gy', 'gz')), parts along dimension 0, may hold values from 0 to 639, as said below
- exports_y: int32 [32, 2, 256], P(('geom', 'gx', 'gy', 'gz')), parts along dimension 0, may hold values from 0 to 639, as said below
- exports_z: int32 [32, 2, 128], P(('geom', 'gx', 'gy', 'gz')), parts along dimension 0, may hold values from 0 to 639, as said below
- face_counts: int32 [32, 6], P(('geom', 'gx', 'gy', 'gz')), parts along dimension 0, may hold values from 1 to 640, as said below
- w_in: bfloat16 [128, 128], replicated, may hold values from -0.5 to 0.5
- w_f1: bfloat16 [50, 128], replicated, may hold values from -1.75 to 1.75
- b_f1: float32 [128], replicated, may hold values from -3 to 3
- w_f2: bfloat16 [128, 128], replicated, may hold values from -0.125 to 0.125
- b_f2: float32 [128], replicated, may hold values from -3 to 3
- w_o1: bfloat16 [128, 128], replicated, may hold values from -0.5 to 0.5
- b_o1: float32 [128], replicated, may hold values from -3 to 3
- w_o2: bfloat16 [128, 128], replicated, may hold values from -0.5 to 0.5
- b_o2: float32 [128], replicated, may hold values from -3 to 3
- w_e1: bfloat16 [128, 64], replicated, may hold values from -0.5 to 0.5
- b_e1: float32 [64], replicated, may hold values from -3 to 3
- w_e2: float32 [64], replicated, may hold values from -1.5 to 1.5
- species_scale: float32 [100], replicated, may hold values from 0.5 to 4
- species_shift: float32 [100], replicated, may hold values from -1 to 1
Outputs:
- energy: float32 [20480], P(('geom', 'gx', 'gy', 'gz')), parts along dimension 0
- forces: float32 [3, 20480], P(None, ('geom', 'gx', 'gy', 'gz')), parts along dimension 1
There are 2 independent parts, one for each index of `geom`. A program takes and returns all parts, laid end to end along the dimension named above; an argument that names none is the same for every part. Nothing has to cross between parts.
Inputs may be any that keep to these rules, and one draw needn't show every extreme that they name: `face_counts`: entry column f is the used length of that face's list: at most 640 for columns 0 and 1, 256 for 2 and 3, 128 for 4 and 5; in every column some domain uses its whole list. `exports_x`: each list row names distinct own atoms. `exports_y`: each list row names distinct own atoms. `exports_z`: each list row names distinct own atoms. `neighbour`: live slots name an own row or a ghost row below the used length of its block; slots beyond the live count hold arbitrary rows. `neighbour_count`: every domain has an atom with all 48 slots live. `displacement`: lengths lie between 0.9 and 4.9.
All inputs are finite; a program needn't handle non-finite values.
Results may differ from a plain program's by a relative error of at most 0.012.
Values may be sent and summed in bfloat16 or wider, within the bound.
A program may use at most 128 MiB of HBM per device.

v0:
```python
import math

import jax
import jax.numpy as jnp
from jax import lax
from jax.experimental import pallas as pl
from jax.experimental.pallas import tpu as pltpu
from jax.sharding import PartitionSpec as P

GAMMA = 10.0
CUTOFF = 5.0
LOG_TWO = math.log(2.0)
LOG2E = 1.0 / LOG_TWO
LANES = 128
UNROLL = 4
PIECES = 4
CHUNK = 256
RADIAL_ROWS = 64
GROUP_ROWS = 24

BF16 = jnp.bfloat16
F32 = jnp.float32


def dot(a, b):
    return jnp.dot(a, b, preferred_element_type=F32)


def dot_nt(a, b):
    return lax.dot_general(a, b, (((1,), (1,)), ((), ())), preferred_element_type=F32)


def split3(value):
    high = value.astype(BF16)
    rest = value - high.astype(F32)
    middle = rest.astype(BF16)
    low = (rest - middle.astype(F32)).astype(BF16)
    return high, middle, low


def softplus_of(value):
    return jnp.maximum(value, 0.0) + jnp.log(1.0 + jnp.exp(-jnp.abs(value)))


def sigmoid_of(value):
    return 1.0 / (1.0 + jnp.exp(-value))


def flip(weight):
    return weight.astype(F32).T.astype(BF16)


def pair_kernel(
    disp_ref,
    index_ref,
    count_ref,
    species_ref,
    scale_ref,
    shift_ref,
    feat_ref,
    table_ref,
    w1_ref,
    b1_ref,
    w2_ref,
    wo1_ref,
    wo2_ref,
    we1_ref,
    bf2_ref,
    bo1_ref,
    bo2_ref,
    be1_ref,
    w_e2_ref,
    energy_ref,
    own_ref,
    spread_ref,
    dist_ref,
    env_ref,
    row_ref,
    s1_ref,
    s2_ref,
    msg_ref,
    gm_ref,
    xj_ref,
    prod_ref,
    sig_ref,
    slope_ref,
    pf_ref,
    piece_ref,
    total_ref,
):
    slots, atoms = index_ref.shape
    width = feat_ref.shape[1]
    piece_rows = piece_ref.shape[1]
    tiles = atoms // LANES
    steps = slots // UNROLL
    span = UNROLL * LANES
    radial = w1_ref.shape[0]

    table_rows = table_ref.shape[1]
    for q in range(PIECES):
        have = max(0, min(piece_rows, table_rows - q * piece_rows))
        band = slice(q * width, (q + 1) * width)
        if have:
            piece_ref[band, 0:have] = table_ref[:, q * piece_rows : q * piece_rows + have]
        if have < piece_rows:
            piece_ref[band, have:piece_rows] = jnp.zeros((width, piece_rows - have), BF16)

    atom_row = lax.broadcasted_iota(jnp.int32, (1, atoms), 1)
    atom_col = lax.broadcasted_iota(jnp.int32, (atoms, 1), 0)
    count_row = count_ref[...].reshape(1, atoms)
    key_row = (count_row * atoms - atom_row).astype(F32)
    count_col = jnp.broadcast_to(count_row.astype(F32), (128, atoms)).T[:, 0:1]
    key_col = count_col * float(atoms) - atom_col.astype(F32)
    rank_col = jnp.sum(jnp.where(key_row > key_col, 1.0, 0.0), axis=1, keepdims=True)
    perm = jnp.where(rank_col == atom_row.astype(F32), 1.0, 0.0).astype(BF16)

    def sort_exact(value):
        high, middle, low = split3(value)
        return dot(high, perm) + dot(middle, perm) + dot(low, perm)

    def unsort_exact(value):
        high, middle, low = split3(value)
        return dot_nt(high, perm) + dot_nt(middle, perm) + dot_nt(low, perm)

    def put(ref, value):
        for s in range(steps):
            ref[s] = value[s * UNROLL : (s + 1) * UNROLL]

    def take(ref):
        return jnp.concatenate([ref[s] for s in range(steps)], axis=0)

    disp = sort_exact(disp_ref[...])
    index = index_ref[...]
    index_high = dot((index >> 7).astype(F32).astype(BF16), perm)
    index_low = dot((index & 127).astype(F32).astype(BF16), perm)
    put(row_ref, index_high * 128.0 + index_low)
    counts = dot(
        jnp.broadcast_to(count_row, (8, atoms)).astype(F32).astype(BF16), perm
    )[0:1]
    kinds = scale_ref.shape[0]
    kind_ids = lax.broadcasted_iota(jnp.int32, (kinds, 1), 0)
    kind_pick = jnp.where(kind_ids == species_ref[...].reshape(1, atoms), 1.0, 0.0).astype(BF16)
    pair_of = jnp.concatenate(
        [
            jnp.broadcast_to(scale_ref[...].reshape(1, kinds), (8, kinds)),
            jnp.broadcast_to(shift_ref[...].reshape(1, kinds), (8, kinds)),
        ],
        axis=0,
    )
    atom_vals = sort_exact(sum(dot(part, kind_pick) for part in split3(pair_of)))
    scale = atom_vals[0:1]
    shift = atom_vals[8:9]
    feat = dot(feat_ref[...].astype(F32).T.astype(BF16), perm)

    dx = disp[0:slots]
    dy = disp[slots : 2 * slots]
    dz = disp[2 * slots : 3 * slots]
    squared = dx * dx + dy * dy + dz * dz
    distance = jnp.sqrt(squared)
    put(dist_ref, distance)
    slot_ids = lax.broadcasted_iota(jnp.int32, (slots, 1), 0).astype(F32)
    live = jnp.where(slot_ids < counts, 1.0, 0.0)
    y = (math.pi / CUTOFF) * distance - 0.5 * math.pi
    y2 = y * y
    sin_y = y * (
        1.0
        + y2
        * (
            -1.0 / 6
            + y2 * (1.0 / 120 + y2 * (-1.0 / 5040 + y2 * (1.0 / 362880 - y2 * (1.0 / 39916800))))
        )
    )
    envelope = (0.5 - 0.5 * sin_y) * live
    put(env_ref, envelope)
    s1_ref[...] = jnp.zeros_like(s1_ref)
    s2_ref[...] = jnp.zeros_like(s2_ref)

    bias = b1_ref[...].reshape(1, width)
    bias_high = bias.astype(BF16).astype(F32)
    bias_middle = (bias - bias_high).astype(BF16).astype(F32)
    w1 = jnp.concatenate(
        [
            w1_ref[...].astype(F32),
            bias_high,
            bias_middle,
            bias - bias_high - bias_middle,
            jnp.zeros((RADIAL_ROWS - radial - 3, width), F32),
        ],
        axis=0,
    )
    w1t = w1.T.astype(BF16)
    radial_col = lax.broadcasted_iota(jnp.int32, (RADIAL_ROWS, 1), 0)
    w1_back = jnp.where(radial_col < radial, w1, 0.0).astype(BF16)
    mu = radial_col.astype(F32) * (CUTOFF / (radial - 1))
    sharp = jnp.where(radial_col < radial, -GAMMA * LOG2E, 0.0)
    w2 = w2_ref[...]
    w2t = flip(w2)

    def column(ref):
        size = ref.shape[0]
        return jnp.broadcast_to(ref[...].reshape(1, size), (128, size)).T[:, 0:1]

    b_f2 = column(bf2_ref) * LOG2E
    b_o1 = column(bo1_ref)
    b_o2 = column(bo2_ref)
    b_e1 = column(be1_ref)
    w_e2 = column(w_e2_ref)

    def lane_row(ref, step, tile):
        return jnp.concatenate(
            [
                ref[step, u : u + 1, tile * LANES : (tile + 1) * LANES]
                for u in range(UNROLL)
            ],
            axis=1,
        )

    sizes = []
    left = piece_rows
    while left > 0:
        sizes.append(min(CHUNK, left))
        left -= sizes[-1]

    def gather(row):
        piece = jnp.zeros_like(row)
        for q in range(1, PIECES):
            piece = piece + jnp.where(row >= float(q * piece_rows), 1.0, 0.0)
        local = row - piece * float(piece_rows)
        parts = []
        start = 0
        for size in sizes:
            inside = (local >= float(start)) & (local < float(start + size))
            spot = jnp.where(inside, local - float(start), -1.0)
            spot = jnp.broadcast_to(spot, (16, span)).astype(BF16)
            lanes = lax.broadcasted_iota(jnp.int32, (16, span), 0).astype(F32)
            for b in range(size // 16):
                ids = (lanes + float(16 * b)).astype(BF16)
                parts.append(
                    jnp.where(ids == spot, jnp.ones((), BF16), jnp.zeros((), BF16))
                )
            start += size
        onehot = jnp.concatenate(parts, axis=0)
        found = dot(piece_ref[...], onehot)
        out = found[0:width]
        for q in range(1, PIECES):
            out = jnp.where(piece == float(q), found[q * width : (q + 1) * width], out)
        return out

    trips = []
    for tile in range(tiles):
        most = jnp.max(counts[:, tile * LANES : (tile + 1) * LANES]).astype(jnp.int32)
        trips.append((most + (UNROLL - 1)) // UNROLL)

    for tile in range(tiles):
        lanes = slice(tile * LANES, (tile + 1) * LANES)
        msg_ref[:, lanes] = jnp.zeros((width, LANES), F32)

        def forward(step, carry, tile=tile, lanes=lanes):
            at = tile * steps + step
            offset = lane_row(dist_ref, step, tile) - mu
            basis = jnp.exp2(sharp * (offset * offset))
            slope_ref[at] = (offset * basis).astype(BF16)
            pre = dot(w1t, basis.astype(BF16))
            grown = jnp.exp2(pre * LOG2E)
            total = 1.0 + grown
            sig_ref[at] = (grown * pl.reciprocal(total, approx=True)).astype(BF16)
            hidden = (jnp.log2(total) - 1.0).astype(BF16)
            filt = dot(w2t, hidden) + b_f2
            xj = gather(lane_row(row_ref, step, tile))
            xj_ref[at] = xj.astype(BF16)
            prod = xj * filt
            prod_ref[at] = prod.astype(BF16)
            weighted = prod * lane_row(env_ref, step, tile)
            part = msg_ref[:, lanes]
            for u in range(UNROLL):
                part = part + weighted[:, u * LANES : (u + 1) * LANES]
            msg_ref[:, lanes] = part
            return carry

        lax.fori_loop(0, trips[tile], forward, 0)

    wo1 = wo1_ref[...]
    wo2 = wo2_ref[...]
    we1 = we1_ref[...]
    message = (msg_ref[...] * LOG_TWO).astype(BF16)
    out_pre = dot(flip(wo1), message) + b_o1
    out_mid = (softplus_of(out_pre) - LOG_TWO).astype(BF16)
    updated = (feat + dot(flip(wo2), out_mid) + b_o2).astype(BF16)
    energy_pre = dot(we1, updated) + b_e1
    soft = softplus_of(energy_pre) - LOG_TWO
    energy = scale * jnp.sum(soft * w_e2, axis=0, keepdims=True) + shift
    grad_head = (scale * w_e2 * sigmoid_of(energy_pre)).astype(BF16)
    grad_update = dot(flip(we1), grad_head).astype(BF16)
    grad_mid = (dot(wo2, grad_update) * sigmoid_of(out_pre)).astype(BF16)
    gm_ref[...] = dot(wo1, grad_mid)

    for tile in range(tiles):
        lanes = slice(tile * LANES, (tile + 1) * LANES)

        def backward(step, carry, tile=tile, lanes=lanes):
            at = tile * steps + step
            grad = gm_ref[:, lanes]
            grad_wide = jnp.concatenate([grad] * UNROLL, axis=1)
            grad_b = grad.astype(BF16)
            grad_b_wide = jnp.concatenate([grad_b] * UNROLL, axis=1)
            mixed = dot(w2, grad_b_wide * xj_ref[at])
            grad_pre = (mixed * sig_ref[at].astype(F32)).astype(BF16)
            grad_basis = dot(w1_back, grad_pre)
            s1 = jnp.sum(grad_basis * slope_ref[at].astype(F32), axis=0, keepdims=True)
            s2 = jnp.sum(grad_wide * prod_ref[at].astype(F32), axis=0, keepdims=True)
            for u in range(UNROLL):
                piece = slice(u * LANES, (u + 1) * LANES)
                s1_ref[step, u : u + 1, lanes] = s1[:, piece]
                s2_ref[step, u : u + 1, lanes] = s2[:, piece]
            return carry

        lax.fori_loop(0, trips[tile], backward, 0)

    cos_y = 1.0 + y2 * (
        -0.5
        + y2
        * (
            1.0 / 24
            + y2
            * (
                -1.0 / 720
                + y2 * (1.0 / 40320 + y2 * (-1.0 / 3628800 + y2 * (1.0 / 479001600)))
            )
        )
    )
    env_slope = (-0.5 * math.pi / CUTOFF * LOG_TWO) * cos_y
    grad_dist = envelope * (-2.0 * GAMMA) * take(s1_ref) + env_slope * take(s2_ref)
    ratio = jnp.where(live > 0.5, grad_dist / distance, 0.0)
    fx = dx * ratio
    fy = dy * ratio
    fz = dz * ratio
    put(pf_ref.at[0], fx)
    put(pf_ref.at[1], fy)
    put(pf_ref.at[2], fz)
    own = jnp.concatenate(
        [jnp.sum(fx, axis=0, keepdims=True), jnp.sum(fy, axis=0, keepdims=True),
         jnp.sum(fz, axis=0, keepdims=True), energy, jnp.zeros((4, atoms), F32)],
        axis=0,
    )
    plain = unsort_exact(own)
    own_ref[...] = plain
    energy_ref[...] = plain[3:4].reshape(atoms)

    total_ref[...] = jnp.zeros_like(total_ref)
    spread_ref[...] = jnp.zeros_like(spread_ref)

    def spread(step, carry):
        group = lax.broadcasted_iota(jnp.int32, (GROUP_ROWS, 1), 0).astype(F32)
        low_ids = lax.broadcasted_iota(jnp.int32, (128, 1), 0).astype(F32)
        total = total_ref[...]
        for u in range(UNROLL):
            row = row_ref[step, u : u + 1, :]
            high = jnp.floor(row * (1.0 / 128))
            low = row - high * 128.0
            here = group == high
            placed = jnp.concatenate(
                [jnp.where(here, -pf_ref[c, step, u : u + 1, :], 0.0) for c in range(3)], axis=0
            ).astype(BF16)
            lower = jnp.where(low_ids == low, 1.0, 0.0).astype(BF16)
            total = total + dot_nt(placed, lower)
        total_ref[...] = total
        return carry

    lax.fori_loop(0, steps, spread, 0)
    for c in range(3):
        spread_ref[:, c, :] = total_ref[c * GROUP_ROWS : (c + 1) * GROUP_ROWS]


def neighbours():
    found = []
    for axis in ("gx", "gy", "gz"):
        size = lax.axis_size(axis)
        place = lax.axis_index(axis)
        found.append({axis: lax.rem(place + 1, size)})
        found.append({axis: lax.rem(place + size - 1, size)})
    return found


def greet(found):
    barrier = pltpu.get_barrier_semaphore()
    for device in found:
        pl.semaphore_signal(
            barrier, inc=1, device_id=device, device_id_type=pl.DeviceIdType.MESH
        )
    pl.semaphore_wait(barrier, len(found))


def picker(list_row, used, atoms):
    lanes = lax.broadcasted_iota(jnp.int32, list_row.shape, 1)
    names = jnp.where(lanes < used, list_row, -1).astype(F32)
    ids = lax.broadcasted_iota(jnp.int32, (atoms, 1), 0).astype(F32)
    return jnp.where(ids == names, 1.0, 0.0).astype(BF16)


FACES = ((0, 1, 1, 0), (0, 0, 0, 1), (1, 1, 3, 2), (1, 0, 2, 3), (2, 1, 5, 4), (2, 0, 4, 5))


def send_kernel(
    feat_ref, w_ref, ex_ref, ey_ref, ez_ref, used_ref, table_ref, stage_ref, send_sem, recv_sem
):
    atoms = feat_ref.shape[0]
    lists = (ex_ref, ey_ref, ez_ref)
    found = neighbours()
    x = dot(feat_ref[...], w_ref[...])
    x_t = x.T.astype(BF16)
    used = used_ref[...]
    greet(found)
    copies = []
    start = 0
    for n, (dim, side, column, to) in enumerate(FACES):
        length = lists[dim].shape[1]
        pick = picker(lists[dim][side : side + 1, :], used[:, column : column + 1], atoms)
        stage_ref[:, start : start + length] = dot(x_t, pick).astype(BF16)
        copy = pltpu.make_async_remote_copy(
            src_ref=stage_ref.at[:, pl.ds(start, length)],
            dst_ref=table_ref.at[:, pl.ds(atoms + start, length)],
            send_sem=send_sem.at[n],
            recv_sem=recv_sem.at[n],
            device_id=found[to],
            device_id_type=pl.DeviceIdType.MESH,
        )
        copy.start()
        copies.append(copy)
        start += length
    table_ref[:, 0:atoms] = x_t
    for copy in copies:
        copy.wait()


def return_kernel(
    own_ref,
    spread_ref,
    ex_ref,
    ey_ref,
    ez_ref,
    used_ref,
    force_ref,
    land_ref,
    send_sem,
    recv_sem,
):
    atoms = force_ref.shape[1]
    lists = (ex_ref, ey_ref, ez_ref)
    found = neighbours()
    greet(found)
    copies = []
    group = atoms // 128
    start = 0
    for n, (dim, side, column, to) in enumerate(FACES):
        length = lists[dim].shape[1] // 128
        copy = pltpu.make_async_remote_copy(
            src_ref=spread_ref.at[pl.ds(group + start, length)],
            dst_ref=land_ref.at[pl.ds(start, length)],
            send_sem=send_sem.at[n],
            recv_sem=recv_sem.at[n],
            device_id=found[to ^ 1],
            device_id_type=pl.DeviceIdType.MESH,
        )
        copy.start()
        copies.append(copy)
        start += length
    total = own_ref[...] + jnp.concatenate([spread_ref[h] for h in range(group)], axis=1)
    used = used_ref[...]
    start = 0
    for n, (dim, side, column, to) in enumerate(FACES):
        length = lists[dim].shape[1] // 128
        pick = picker(lists[dim][side : side + 1, :], used[:, column : column + 1], atoms)
        copies[n].wait()
        values = jnp.concatenate([land_ref[start + h] for h in range(length)], axis=1)
        high, middle, low = split3(values)
        total = total + dot_nt(high, pick) + dot_nt(middle, pick) + dot_nt(low, pick)
        start += length
    force_ref[...] = total[0:3]


def body(
    features,
    displacement,
    neighbour,
    neighbour_count,
    species,
    exports_x,
    exports_y,
    exports_z,
    face_counts,
    w_in,
    w_f1,
    b_f1,
    w_f2,
    b_f2,
    w_o1,
    b_o1,
    w_o2,
    b_o2,
    w_e1,
    b_e1,
    w_e2,
    species_scale,
    species_shift,
):
    atom_rows, width = features.shape
    slot_count = neighbour.shape[0] // atom_rows
    used_counts = face_counts[0]
    vmem = pl.BlockSpec(memory_space=pltpu.VMEM)
    lists = (exports_x[0], exports_y[0], exports_z[0])
    ghost_rows = sum(2 * one.shape[1] for one in lists)
    table_rows = atom_rows + ghost_rows
    table_t = pl.pallas_call(
        send_kernel,
        out_shape=jax.ShapeDtypeStruct((width, table_rows), BF16),
        in_specs=[vmem] * 6,
        out_specs=vmem,
        scratch_shapes=[
            pltpu.VMEM((width, ghost_rows), BF16),
            pltpu.SemaphoreType.DMA((6,)),
            pltpu.SemaphoreType.DMA((6,)),
        ],
        compiler_params=pltpu.CompilerParams(
            collective_id=0, has_side_effects=True, vmem_limit_bytes=32 * 1024 * 1024
        ),
    )(features, w_in, *lists, face_counts)
    piece_rows = -(-table_rows // (PIECES * CHUNK)) * CHUNK
    disp_t = (
        displacement.reshape(3, atom_rows, slot_count).transpose(0, 2, 1).reshape(-1, atom_rows)
    )
    index_t = neighbour.reshape(atom_rows, slot_count).T
    steps = slot_count // UNROLL * (atom_rows // LANES)
    span = UNROLL * LANES
    energy, own_force, spread = pl.pallas_call(
        pair_kernel,
        out_shape=(
            jax.ShapeDtypeStruct((atom_rows,), F32),
            jax.ShapeDtypeStruct((8, atom_rows), F32),
            jax.ShapeDtypeStruct((GROUP_ROWS, 8, 128), F32),
        ),
        in_specs=[vmem] * 19,
        out_specs=(vmem, vmem, vmem),
        scratch_shapes=[
            pltpu.VMEM((slot_count // UNROLL, UNROLL, atom_rows), F32),
            pltpu.VMEM((slot_count // UNROLL, UNROLL, atom_rows), F32),
            pltpu.VMEM((slot_count // UNROLL, UNROLL, atom_rows), F32),
            pltpu.VMEM((slot_count // UNROLL, UNROLL, atom_rows), F32),
            pltpu.VMEM((slot_count // UNROLL, UNROLL, atom_rows), F32),
            pltpu.VMEM((width, atom_rows), F32),
            pltpu.VMEM((width, atom_rows), F32),
            pltpu.VMEM((steps, width, span), BF16),
            pltpu.VMEM((steps, width, span), BF16),
            pltpu.VMEM((steps, width, span), BF16),
            pltpu.VMEM((steps, RADIAL_ROWS, span), BF16),
            pltpu.VMEM((3, slot_count // UNROLL, UNROLL, atom_rows), F32),
            pltpu.VMEM((PIECES * width, piece_rows), BF16),
            pltpu.VMEM((3 * GROUP_ROWS, 128), F32),
        ],
        compiler_params=pltpu.CompilerParams(vmem_limit_bytes=56 * 1024 * 1024),
        cost_estimate=pl.CostEstimate(
            flops=30_000_000_000, bytes_accessed=4_000_000, transcendentals=16_000_000
        ),
    )(
        disp_t,
        index_t,
        neighbour_count,
        species,
        species_scale,
        species_shift,
        features,
        table_t,
        w_f1,
        b_f1,
        w_f2,
        w_o1,
        w_o2,
        w_e1.T,
        b_f2,
        b_o1,
        b_o2,
        b_e1,
        w_e2,
    )
    forces = pl.pallas_call(
        return_kernel,
        out_shape=jax.ShapeDtypeStruct((3, atom_rows), F32),
        in_specs=[vmem] * 6,
        out_specs=vmem,
        scratch_shapes=[
            pltpu.VMEM((ghost_rows // 128, 8, 128), F32),
            pltpu.SemaphoreType.DMA((6,)),
            pltpu.SemaphoreType.DMA((6,)),
        ],
        compiler_params=pltpu.CompilerParams(
            collective_id=1, has_side_effects=True, vmem_limit_bytes=32 * 1024 * 1024
        ),
    )(own_force, spread, *lists, face_counts)
    return (energy, forces)


def solution(mesh):
    both = ("geom", "gx", "gy", "gz")
    return jax.shard_map(
        body,
        mesh=mesh,
        in_specs=(
            P(both, None),
            P(None, both),
            P(both),
            P(both),
            P(both),
            P(both, None, None),
            P(both, None, None),
            P(both, None, None),
            P(both, None),
        )
        + (P(),) * 14,
        out_specs=(P(both), P(None, both)),
        check_vma=False,
    )
```

profile of v0, /device:TPU:0, one launch (start us, length us, event | category | flops | bytes accessed | tf_op | source)
XLA Modules:
  0.0 95.5 jit_solution(17803901921370370103)
XLA Ops:
  0.6 1.5 %reshape.13 = f32[3,640,48]{2,1,0:T(8,128)S(1)} reshape(f32[3,30720]{1,0:T(4,128)} %param.24) | data formatting | bytes 737280 | tf_op jit(solution)/shard_map/reshape | solution.py:529
  2.1 0.0 copy-start.9
  2.2 1.1 %copy.26 = f32[3,48,640]{2,1,0:T(8,128)} copy(f32[3,48,640]{1,2,0:T(8,128)S(1)} %bitcast.13) | data formatting | bytes 737280 | tf_op jit(solution)/shard_map/transpose | solution.py:529
  3.2 0.0 copy-done.9
  3.2 0.2 reshape.15
  3.4 0.0 copy-start.1
  3.4 0.0 copy-start.3
  3.4 0.0 copy-start.7
  3.4 0.8 copy.27
  4.2 0.0 copy-start.4
  4.2 0.1 copy-done.1
  4.3 0.0 copy-done.3
  4.3 0.0 copy-done.7
  4.3 0.6 copy-done.4
  4.9 0.0 copy-done.6
  4.9 0.0 copy-done.8
  4.9 13.2 %shard_map.230.table_ref = bf16[128,2688]{1,0:T(8,128)(2,1)S(1)} custom-call(bf16[640,128]{1,0:T(8,128)(2,1)S(1)} %copy-done.1, bf16[128,128]{1,0:T(8,128)(2,1)S(1)} %copy-done.3, s32[2,640]{1,0:T(2,128)S(1)} %bitcast.7, s32[2,256]{1,0:T(2,128)S(1)} %bitcast.9, s32[2,128]{1,0:T(2,128)S(1)} %bitcast.11, s32[1,6]{1,0:T(1,128)S(1)} %copy-done.8), custom_call_target="tpu_custom_call" | custom-call | tf_op jit(solution)/shard_map/pallas_call | solution.py:513
  18.1 0.0 copy-start
  18.1 0.8 copy-done
  19.0 64.9 %shard_map.231 = (f32[640]{0:T(1024)}, f32[8,640]{1,0:T(8,128)}, f32[24,8,128]{2,1,0:T(8,128)}) custom-call(f32[144,640]{1,0:T(8,128)} %bitcast.14, s32[48,640]{1,0:T(8,128)} %bitcast.15, s32[640]{0:T(1024)} %count_ref.1, s32[640]{0:T(1024)} %species_ref.1, f32[100]{0:T(128)} %scale_ref.1, f32[100]{0:T(128)} %shift_ref.1, bf16[640,128]{1,0:T(8,128)(2,1)} %feat_ref.3, ...), custom_call_target="tpu_custom_call" | custom-call | flops 30000001024 | bytes 4000000 | tf_op jit(solution)/shard_map/pallas_call | solution.py:534
  83.8 0.9 copy-done.2
  84.7 0.7 copy-done.5
  85.4 9.4 %shard_map.232 = f32[3,640]{1,0:T(4,128)S(1)} custom-call(f32[8,640]{1,0:T(8,128)S(1)} %copy-done.5, f32[24,8,128]{2,1,0:T(8,128)S(1)} %copy-done.2, s32[2,640]{1,0:T(2,128)S(1)} %bitcast.8, s32[2,256]{1,0:T(2,128)S(1)} %bitcast.10, s32[2,128]{1,0:T(2,128)S(1)} %bitcast.12, s32[1,6]{1,0:T(1,128)S(1)} %copy-done.8), custom_call_target="tpu_custom_call" | custom-call | tf_op jit(solution)/shard_map/pallas_call | solution.py:584
  94.9 0.6 copy.29
  (4 shorter events, 0.0 us)
Async XLA Ops:
  2.1 1.1 %copy-start.9 = (s32[30720]{0:T(1024)S(1)}, s32[30720]{0:T(1024)}, u32[]{:S(2)}) copy-start(s32[30720]{0:T(1024)} %param.25) | copy-start | bytes 368644
  3.4 0.9 copy-start.1
  3.4 0.9 copy-start.3
  3.4 0.9 copy-start.7
  4.2 0.7 copy-start.4
  4.2 0.7 copy-start.6
  4.2 0.7 copy-start.8
  18.1 0.8 copy-start
  83.8 0.9 copy-start.2
  84.7 0.7 copy-start.5
where the time goes:
time: 95.8 us; the launch traced here: 95.5 us
  Pallas kernels  87.5 us (91%)
  local copies, waits for them, and re-layouts  7.3 us (8%)
    pallas_call x1, Pallas kernels, body(): pl.pallas_call(pair_kernel, out_shape=(jax.ShapeDtypeStruct((atom_rows,),...  64.9 us
    pallas_call x1, Pallas kernels, body(): pl.pallas_call(send_kernel, out_shape=jax.ShapeDtypeStruct((width, table_...  13.2 us
    pallas_call x1, Pallas kernels, body(): pl.pallas_call(return_kernel, out_shape=jax.ShapeDtypeStruct((3, atom_row...  9.42 us
    unnamed x21, local copies, waits for them, and re-layouts  3.8 us

commit v1 on v0

--- a/solution.py
+++ b/solution.py
@@ -13,10 +13,9 @@
 LOG2E = 1.0 / LOG_TWO
 LANES = 128
 UNROLL = 4
-PIECES = 4
 CHUNK = 256
 RADIAL_ROWS = 64
-GROUP_ROWS = 24
+GROUP_ROWS = 32
 
 BF16 = jnp.bfloat16
 F32 = jnp.float32
@@ -76,34 +75,34 @@
     dist_ref,
     env_ref,
     row_ref,
-    s1_ref,
-    s2_ref,
+    near_ref,
+    far_ref,
+    disp3_ref,
     msg_ref,
     gm_ref,
+    own3_ref,
     xj_ref,
     prod_ref,
     sig_ref,
     slope_ref,
-    pf_ref,
-    piece_ref,
+    hid_a_ref,
+    hid_b_ref,
+    filt_a_ref,
+    filt_b_ref,
+    found_a_ref,
+    found_b_ref,
+    back_a_ref,
+    back_b_ref,
     total_ref,
 ):
     slots, atoms = index_ref.shape
     width = feat_ref.shape[1]
-    piece_rows = piece_ref.shape[1]
     tiles = atoms // LANES
     steps = slots // UNROLL
     span = UNROLL * LANES
     radial = w1_ref.shape[0]
-
     table_rows = table_ref.shape[1]
-    for q in range(PIECES):
-        have = max(0, min(piece_rows, table_rows - q * piece_rows))
-        band = slice(q * width, (q + 1) * width)
-        if have:
-            piece_ref[band, 0:have] = table_ref[:, q * piece_rows : q * piece_rows + have]
-        if have < piece_rows:
-            piece_ref[band, have:piece_rows] = jnp.zeros((width, piece_rows - have), BF16)
+    idle = tiles * steps
 
     atom_row = lax.broadcasted_iota(jnp.int32, (1, atoms), 1)
     atom_col = lax.broadcasted_iota(jnp.int32, (atoms, 1), 0)
@@ -123,11 +122,12 @@
         return dot_nt(high, perm) + dot_nt(middle, perm) + dot_nt(low, perm)
 
     def put(ref, value):
-        for s in range(steps):
-            ref[s] = value[s * UNROLL : (s + 1) * UNROLL]
-
-    def take(ref):
-        return jnp.concatenate([ref[s] for s in range(steps)], axis=0)
+        for tile in range(tiles):
+            for s in range(steps):
+                ref[tile * steps + s] = value[
+                    s * UNROLL : (s + 1) * UNROLL, tile * LANES : (tile + 1) * LANES
+                ]
+        ref[idle] = jnp.zeros((UNROLL, LANES), F32)
 
     disp = sort_exact(disp_ref[...])
     index = index_ref[...]
@@ -172,8 +172,24 @@
     )
     envelope = (0.5 - 0.5 * sin_y) * live
     put(env_ref, envelope)
-    s1_ref[...] = jnp.zeros_like(s1_ref)
-    s2_ref[...] = jnp.zeros_like(s2_ref)
+    cos_y = 1.0 + y2 * (
+        -0.5
+        + y2
+        * (
+            1.0 / 24
+            + y2
+            * (
+                -1.0 / 720
+                + y2 * (1.0 / 40320 + y2 * (-1.0 / 3628800 + y2 * (1.0 / 479001600)))
+            )
+        )
+    )
+    inverse = live / distance
+    put(near_ref, envelope * (-2.0 * GAMMA) * inverse)
+    put(far_ref, (-0.5 * math.pi / CUTOFF * LOG_TWO) * cos_y * inverse)
+    put(disp3_ref.at[0], dx)
+    put(disp3_ref.at[1], dy)
+    put(disp3_ref.at[2], dz)
 
     bias = b1_ref[...].reshape(1, width)
     bias_high = bias.astype(BF16).astype(F32)
@@ -206,83 +222,100 @@
     b_e1 = column(be1_ref)
     w_e2 = column(w_e2_ref)
 
-    def lane_row(ref, step, tile):
-        return jnp.concatenate(
-            [
-                ref[step, u : u + 1, tile * LANES : (tile + 1) * LANES]
-                for u in range(UNROLL)
-            ],
-            axis=1,
-        )
-
-    sizes = []
-    left = piece_rows
-    while left > 0:
-        sizes.append(min(CHUNK, left))
-        left -= sizes[-1]
+    def lane_row(ref, at):
+        return jnp.concatenate([ref[at, u : u + 1, :] for u in range(UNROLL)], axis=1)
+
+    ends = []
+    items = jnp.zeros((), jnp.int32)
+    for tile in range(tiles):
+        most = jnp.max(counts[:, tile * LANES : (tile + 1) * LANES]).astype(jnp.int32)
+        items = items + (most + (UNROLL - 1)) // UNROLL
+        ends.append(items)
+    rounds = (items + 1) // 2
+
+    def place(item):
+        tile = jnp.zeros((), jnp.int32)
+        first = jnp.zeros((), jnp.int32)
+        for end in ends[:-1]:
+            past = item >= end
+            tile = tile + past.astype(jnp.int32)
+            first = jnp.where(past, end, first)
+        at = jnp.where((item >= 0) & (item < items), tile * steps + item - first, idle)
+        return tile, at
 
     def gather(row):
-        piece = jnp.zeros_like(row)
-        for q in range(1, PIECES):
-            piece = piece + jnp.where(row >= float(q * piece_rows), 1.0, 0.0)
-        local = row - piece * float(piece_rows)
         parts = []
-        start = 0
-        for size in sizes:
-            inside = (local >= float(start)) & (local < float(start + size))
-            spot = jnp.where(inside, local - float(start), -1.0)
-            spot = jnp.broadcast_to(spot, (16, span)).astype(BF16)
+        for start in range(0, table_rows, CHUNK):
+            size = min(CHUNK, table_rows - start)
+            spot = jnp.broadcast_to(row - float(start), (16, span)).astype(BF16)
             lanes = lax.broadcasted_iota(jnp.int32, (16, span), 0).astype(F32)
             for b in range(size // 16):
                 ids = (lanes + float(16 * b)).astype(BF16)
                 parts.append(
                     jnp.where(ids == spot, jnp.ones((), BF16), jnp.zeros((), BF16))
                 )
-            start += size
-        onehot = jnp.concatenate(parts, axis=0)
-        found = dot(piece_ref[...], onehot)
-        out = found[0:width]
-        for q in range(1, PIECES):
-            out = jnp.where(piece == float(q), found[q * width : (q + 1) * width], out)
-        return out
-
-    trips = []
-    for tile in range(tiles):
-        most = jnp.max(counts[:, tile * LANES : (tile + 1) * LANES]).astype(jnp.int32)
-        trips.append((most + (UNROLL - 1)) // UNROLL)
-
-    for tile in range(tiles):
-        lanes = slice(tile * LANES, (tile + 1) * LANES)
-        msg_ref[:, lanes] = jnp.zeros((width, LANES), F32)
-
-        def forward(step, carry, tile=tile, lanes=lanes):
-            at = tile * steps + step
-            offset = lane_row(dist_ref, step, tile) - mu
-            basis = jnp.exp2(sharp * (offset * offset))
-            slope_ref[at] = (offset * basis).astype(BF16)
-            pre = dot(w1t, basis.astype(BF16))
-            grown = jnp.exp2(pre * LOG2E)
-            total = 1.0 + grown
-            sig_ref[at] = (grown * pl.reciprocal(total, approx=True)).astype(BF16)
-            hidden = (jnp.log2(total) - 1.0).astype(BF16)
-            filt = dot(w2t, hidden) + b_f2
-            xj = gather(lane_row(row_ref, step, tile))
-            xj_ref[at] = xj.astype(BF16)
-            prod = xj * filt
-            prod_ref[at] = prod.astype(BF16)
-            weighted = prod * lane_row(env_ref, step, tile)
-            part = msg_ref[:, lanes]
-            for u in range(UNROLL):
-                part = part + weighted[:, u * LANES : (u + 1) * LANES]
-            msg_ref[:, lanes] = part
-            return carry
-
-        lax.fori_loop(0, trips[tile], forward, 0)
+        return dot(table_ref[...], jnp.concatenate(parts, axis=0))
+
+    def radial_dot(at):
+        offset = lane_row(dist_ref, at) - mu
+        basis = jnp.exp2(sharp * (offset * offset))
+        return (offset * basis).astype(BF16), dot(w1t, basis.astype(BF16))
+
+    def activate(pre):
+        grown = jnp.exp2(pre * LOG2E)
+        total = 1.0 + grown
+        sig = (grown * pl.reciprocal(total, approx=True)).astype(BF16)
+        return sig, (jnp.log2(total) - 1.0).astype(BF16)
+
+    def begin(item, hid_ref):
+        slope, pre = radial_dot(place(item)[1])
+        slope_ref[item + 1] = slope
+        sig, hidden = activate(pre)
+        sig_ref[item + 1] = sig
+        hid_ref[...] = hidden
+
+    def finish(item, filt_ref, found_ref):
+        tile, at = place(item)
+        prod = found_ref[...] * filt_ref[...]
+        prod_ref[item + 1] = prod.astype(BF16)
+        weighted = prod * lane_row(env_ref, at)
+        part = msg_ref[tile]
+        for u in range(UNROLL):
+            part = part + weighted[:, u * LANES : (u + 1) * LANES]
+        msg_ref[tile] = part
+
+    def forward(item, hid_ref, next_ref, filt_ref, found_ref, last_filt_ref, last_found_ref):
+        filt = dot(w2t, hid_ref[...]) + b_f2
+        slope, pre = radial_dot(place(item + 1)[1])
+        slope_ref[item + 2] = slope
+        found = gather(lane_row(row_ref, place(item)[1]))
+        sig, hidden = activate(pre)
+        sig_ref[item + 2] = sig
+        next_ref[...] = hidden
+        finish(item - 1, last_filt_ref, last_found_ref)
+        filt_ref[...] = filt
+        found_ref[...] = found
+        xj_ref[item + 1] = found.astype(BF16)
+
+    msg_ref[...] = jnp.zeros_like(msg_ref)
+    filt_b_ref[...] = jnp.zeros_like(filt_b_ref)
+    found_b_ref[...] = jnp.zeros_like(found_b_ref)
+    begin(jnp.zeros((), jnp.int32), hid_a_ref)
+
+    def forward_round(turn, carry):
+        item = 2 * turn
+        forward(item, hid_a_ref, hid_b_ref, filt_a_ref, found_a_ref, filt_b_ref, found_b_ref)
+        forward(item + 1, hid_b_ref, hid_a_ref, filt_b_ref, found_b_ref, filt_a_ref, found_a_ref)
+        return carry
+
+    lax.fori_loop(0, rounds, forward_round, 0)
+    finish(2 * rounds - 1, filt_b_ref, found_b_ref)
 
     wo1 = wo1_ref[...]
     wo2 = wo2_ref[...]
     we1 = we1_ref[...]
-    message = (msg_ref[...] * LOG_TWO).astype(BF16)
+    message = jnp.concatenate([msg_ref[t] for t in range(tiles)], axis=1)
+    message = (message * LOG_TWO).astype(BF16)
     out_pre = dot(flip(wo1), message) + b_o1
     out_mid = (softplus_of(out_pre) - LOG_TWO).astype(BF16)
     updated = (feat + dot(flip(wo2), out_mid) + b_o2).astype(BF16)
@@ -292,83 +325,78 @@
     grad_head = (scale * w_e2 * sigmoid_of(energy_pre)).astype(BF16)
     grad_update = dot(flip(we1), grad_head).astype(BF16)
     grad_mid = (dot(wo2, grad_update) * sigmoid_of(out_pre)).astype(BF16)
-    gm_ref[...] = dot(wo1, grad_mid)
-
+    grad_message = dot(wo1, grad_mid)
     for tile in range(tiles):
-        lanes = slice(tile * LANES, (tile + 1) * LANES)
-
-        def backward(step, carry, tile=tile, lanes=lanes):
-            at = tile * steps + step
-            grad = gm_ref[:, lanes]
-            grad_wide = jnp.concatenate([grad] * UNROLL, axis=1)
-            grad_b = grad.astype(BF16)
-            grad_b_wide = jnp.concatenate([grad_b] * UNROLL, axis=1)
-            mixed = dot(w2, grad_b_wide * xj_ref[at])
-            grad_pre = (mixed * sig_ref[at].astype(F32)).astype(BF16)
-            grad_basis = dot(w1_back, grad_pre)
-            s1 = jnp.sum(grad_basis * slope_ref[at].astype(F32), axis=0, keepdims=True)
-            s2 = jnp.sum(grad_wide * prod_ref[at].astype(F32), axis=0, keepdims=True)
+        gm_ref[tile] = grad_message[:, tile * LANES : (tile + 1) * LANES]
+
+    total_ref[...] = jnp.zeros_like(total_ref)
+    own3_ref[...] = jnp.zeros_like(own3_ref)
+    back_b_ref[...] = jnp.zeros_like(back_b_ref)
+    prod_ref[0] = jnp.zeros((width, span), BF16)
+    slope_ref[0] = jnp.zeros((RADIAL_ROWS, span), BF16)
+
+    def settle(item, back_ref):
+        tile, at = place(item)
+        grad_basis = dot(w1_back, back_ref[...])
+        grad_wide = jnp.concatenate([gm_ref[tile]] * UNROLL, axis=1)
+        s1 = jnp.sum(grad_basis * slope_ref[item + 1].astype(F32), axis=0, keepdims=True)
+        s2 = jnp.sum(grad_wide * prod_ref[item + 1].astype(F32), axis=0, keepdims=True)
+        ratio = s1 * lane_row(near_ref, at) + s2 * lane_row(far_ref, at)
+        row = lane_row(row_ref, at)
+        high = jnp.floor(row * (1.0 / 128))
+        low = row - high * 128.0
+        wide = (16, span)
+        high_b = jnp.broadcast_to(high, wide).astype(BF16)
+        low_b = jnp.broadcast_to(low, wide).astype(BF16)
+        lanes = lax.broadcasted_iota(jnp.int32, wide, 0).astype(F32)
+        ids = [(lanes + float(16 * b)).astype(BF16) for b in range(8)]
+        lower = jnp.concatenate(
+            [jnp.where(one == low_b, jnp.ones((), BF16), jnp.zeros((), BF16)) for one in ids],
+            axis=0,
+        )
+        here = [ids[b] == high_b for b in range(GROUP_ROWS // 16)]
+        placed = []
+        for c in range(3):
+            force = ratio * lane_row(disp3_ref.at[c], at)
+            part = own3_ref[tile, c : c + 1, :]
             for u in range(UNROLL):
-                piece = slice(u * LANES, (u + 1) * LANES)
-                s1_ref[step, u : u + 1, lanes] = s1[:, piece]
-                s2_ref[step, u : u + 1, lanes] = s2[:, piece]
-            return carry
-
-        lax.fori_loop(0, trips[tile], backward, 0)
-
-    cos_y = 1.0 + y2 * (
-        -0.5
-        + y2
-        * (
-            1.0 / 24
-            + y2
-            * (
-                -1.0 / 720
-                + y2 * (1.0 / 40320 + y2 * (-1.0 / 3628800 + y2 * (1.0 / 479001600)))
-            )
-        )
-    )
-    env_slope = (-0.5 * math.pi / CUTOFF * LOG_TWO) * cos_y
-    grad_dist = envelope * (-2.0 * GAMMA) * take(s1_ref) + env_slope * take(s2_ref)
-    ratio = jnp.where(live > 0.5, grad_dist / distance, 0.0)
-    fx = dx * ratio
-    fy = dy * ratio
-    fz = dz * ratio
-    put(pf_ref.at[0], fx)
-    put(pf_ref.at[1], fy)
-    put(pf_ref.at[2], fz)
+                part = part + force[:, u * LANES : (u + 1) * LANES]
+            own3_ref[tile, c : c + 1, :] = part
+            minus = jnp.broadcast_to(-force, wide).astype(BF16)
+            placed += [jnp.where(mask, minus, jnp.zeros((), BF16)) for mask in here]
+        total_ref[...] = total_ref[...] + dot_nt(jnp.concatenate(placed, axis=0), lower)
+
+    def backward(item, back_ref, last_ref):
+        tile, at = place(item)
+        grad_b = gm_ref[tile].astype(BF16)
+        grad_b_wide = jnp.concatenate([grad_b] * UNROLL, axis=1)
+        mixed = dot(w2, grad_b_wide * xj_ref[item + 1])
+        settle(item - 1, last_ref)
+        back_ref[...] = (mixed * sig_ref[item + 1].astype(F32)).astype(BF16)
+
+    def backward_round(turn, carry):
+        item = 2 * turn
+        backward(item, back_a_ref, back_b_ref)
+        backward(item + 1, back_b_ref, back_a_ref)
+        return carry
+
+    lax.fori_loop(0, rounds, backward_round, 0)
+    settle(2 * rounds - 1, back_b_ref)
+
     own = jnp.concatenate(
-        [jnp.sum(fx, axis=0, keepdims=True), jnp.sum(fy, axis=0, keepdims=True),
-         jnp.sum(fz, axis=0, keepdims=True), energy, jnp.zeros((4, atoms), F32)],
+        [
+            jnp.concatenate([own3_ref[t, 0:3, :] for t in range(tiles)], axis=1),
+            energy,
+            jnp.zeros((4, atoms), F32),
+        ],
         axis=0,
     )
     plain = unsort_exact(own)
     own_ref[...] = plain
     energy_ref[...] = plain[3:4].reshape(atoms)
-
-    total_ref[...] = jnp.zeros_like(total_ref)
     spread_ref[...] = jnp.zeros_like(spread_ref)
-
-    def spread(step, carry):
-        group = lax.broadcasted_iota(jnp.int32, (GROUP_ROWS, 1), 0).astype(F32)
-        low_ids = lax.broadcasted_iota(jnp.int32, (128, 1), 0).astype(F32)
-        total = total_ref[...]
-        for u in range(UNROLL):
-            row = row_ref[step, u : u + 1, :]
-            high = jnp.floor(row * (1.0 / 128))
-            low = row - high * 128.0
-            here = group == high
-            placed = jnp.concatenate(
-                [jnp.where(here, -pf_ref[c, step, u : u + 1, :], 0.0) for c in range(3)], axis=0
-            ).astype(BF16)
-            lower = jnp.where(low_ids == low, 1.0, 0.0).astype(BF16)
-            total = total + dot_nt(placed, lower)
-        total_ref[...] = total
-        return carry
-
-    lax.fori_loop(0, steps, spread, 0)
     for c in range(3):
-        spread_ref[:, c, :] = total_ref[c * GROUP_ROWS : (c + 1) * GROUP_ROWS]
+        spread_ref[:, c, :] = total_ref[c * GROUP_ROWS : c * GROUP_ROWS + spread_ref.shape[0]]
 
 
 def neighbours():
@@ -524,36 +552,41 @@
             collective_id=0, has_side_effects=True, vmem_limit_bytes=32 * 1024 * 1024
         ),
     )(features, w_in, *lists, face_counts)
-    piece_rows = -(-table_rows // (PIECES * CHUNK)) * CHUNK
     disp_t = (
         displacement.reshape(3, atom_rows, slot_count).transpose(0, 2, 1).reshape(-1, atom_rows)
     )
     index_t = neighbour.reshape(atom_rows, slot_count).T
     steps = slot_count // UNROLL * (atom_rows // LANES)
+    tiles = atom_rows // LANES
+    groups = table_rows // 128
     span = UNROLL * LANES
     energy, own_force, spread = pl.pallas_call(
         pair_kernel,
         out_shape=(
             jax.ShapeDtypeStruct((atom_rows,), F32),
             jax.ShapeDtypeStruct((8, atom_rows), F32),
-            jax.ShapeDtypeStruct((GROUP_ROWS, 8, 128), F32),
+            jax.ShapeDtypeStruct((groups, 8, 128), F32),
         ),
         in_specs=[vmem] * 19,
         out_specs=(vmem, vmem, vmem),
-        scratch_shapes=[
-            pltpu.VMEM((slot_count // UNROLL, UNROLL, atom_rows), F32),
-            pltpu.VMEM((slot_count // UNROLL, UNROLL, atom_rows), F32),
-            pltpu.VMEM((slot_count // UNROLL, UNROLL, atom_rows), F32),
-            pltpu.VMEM((slot_count // UNROLL, UNROLL, atom_rows), F32),
-            pltpu.VMEM((slot_count // UNROLL, UNROLL, atom_rows), F32),
-            pltpu.VMEM((width, atom_rows), F32),
-            pltpu.VMEM((width, atom_rows), F32),
-            pltpu.VMEM((steps, width, span), BF16),
-            pltpu.VMEM((steps, width, span), BF16),
-            pltpu.VMEM((steps, width, span), BF16),
-            pltpu.VMEM((steps, RADIAL_ROWS, span), BF16),
-            pltpu.VMEM((3, slot_count // UNROLL, UNROLL, atom_rows), F32),
-            pltpu.VMEM((PIECES * width, piece_rows), BF16),
+        scratch_shapes=[pltpu.VMEM((steps + 1, UNROLL, LANES), F32)] * 5
+        + [
+            pltpu.VMEM((3, steps + 1, UNROLL, LANES), F32),
+            pltpu.VMEM((tiles, width, LANES), F32),
+            pltpu.VMEM((tiles, width, LANES), F32),
+            pltpu.VMEM((tiles, 8, LANES), F32),
+            pltpu.VMEM((steps + 3, width, span), BF16),
+            pltpu.VMEM((steps + 3, width, span), BF16),
+            pltpu.VMEM((steps + 3, width, span), BF16),
+            pltpu.VMEM((steps + 3, RADIAL_ROWS, span), BF16),
+            pltpu.VMEM((width, span), BF16),
+            pltpu.VMEM((width, span), BF16),
+            pltpu.VMEM((width, span), F32),
+            pltpu.VMEM((width, span), F32),
+            pltpu.VMEM((width, span), F32),
+            pltpu.VMEM((width, span), F32),
+            pltpu.VMEM((width, span), BF16),
+            pltpu.VMEM((width, span), BF16),
             pltpu.VMEM((3 * GROUP_ROWS, 128), F32),
         ],
         compiler_params=pltpu.CompilerParams(vmem_limit_bytes=56 * 1024 * 1024),

time: 95.8 us -> 75.3 us (0.79)
  Pallas kernels: 87.5 us -> 66.9 us
    pallas_call x1, Pallas kernels: 64.9 us -> 44.3 us  [body(): pl.pallas_call(pair_kernel, out_shape=(jax.ShapeDtypeStruct((atom_rows,),...]
where the time goes in v1:
time: 75.3 us; the launch traced here: 74.9 us
  Pallas kernels  66.9 us (89%)
  local copies, waits for them, and re-layouts  7.29 us (10%)
    pallas_call x1, Pallas kernels, body(): pl.pallas_call(pair_kernel, out_shape=(jax.ShapeDtypeStruct((atom_rows,),...  44.3 us
    pallas_call x1, Pallas kernels, body(): pl.pallas_call(send_kernel, out_shape=jax.ShapeDtypeStruct((width, table_...  13.2 us
    pallas_call x1, Pallas kernels, body(): pl.pallas_call(return_kernel, out_shape=jax.ShapeDtypeStruct((3, atom_row...  9.42 us
    unnamed x21, local copies, waits for them, and re-layouts  3.79 us

profile of v1, /device:TPU:0, one launch (start us, length us, event | category | flops | bytes accessed | tf_op | source)
XLA Modules:
  0.0 74.9 jit_solution(15661995247867352125)
XLA Ops:
  0.6 1.5 %reshape.13 = f32[3,640,48]{2,1,0:T(8,128)S(1)} reshape(f32[3,30720]{1,0:T(4,128)} %param.24) | data formatting | bytes 737280 | tf_op jit(solution)/shard_map/reshape | solution.py:556
  2.1 0.0 copy-start.9
  2.2 1.1 %copy.26 = f32[3,48,640]{2,1,0:T(8,128)} copy(f32[3,48,640]{1,2,0:T(8,128)S(1)} %bitcast.13) | data formatting | bytes 737280 | tf_op jit(solution)/shard_map/transpose | solution.py:556
  3.2 0.0 copy-done.9
  3.2 0.2 reshape.15
  3.4 0.0 copy-start.1
  3.4 0.0 copy-start.3
  3.4 0.0 copy-start.7
  3.4 0.8 %copy.27 = s32[640,48]{0,1:T(8,128)} copy(s32[640,48]{1,0:T(8,128)S(1)} %reshape.15) | data formatting | bytes 245760 | tf_op jit(solution)/shard_map/reshape | solution.py:558
  4.2 0.0 copy-start.4
  4.2 0.1 copy-done.1
  4.3 0.0 copy-done.3
  4.3 0.0 copy-done.7
  4.3 0.6 copy-done.4
  4.9 0.0 copy-done.6
  4.9 0.0 copy-done.8
  4.9 13.2 %shard_map.230.table_ref = bf16[128,2688]{1,0:T(8,128)(2,1)S(1)} custom-call(bf16[640,128]{1,0:T(8,128)(2,1)S(1)} %copy-done.1, bf16[128,128]{1,0:T(8,128)(2,1)S(1)} %copy-done.3, s32[2,640]{1,0:T(2,128)S(1)} %bitcast.7, s32[2,256]{1,0:T(2,128)S(1)} %bitcast.9, s32[2,128]{1,0:T(2,128)S(1)} %bitcast.11, s32[1,6]{1,0:T(1,128)S(1)} %copy-done.8), custom_call_target="tpu_custom_call" | custom-call | tf_op jit(solution)/shard_map/pallas_call | solution.py:541
  18.1 0.0 copy-start
  18.1 0.8 %copy-done = bf16[128,2688]{1,0:T(8,128)(2,1)} copy-done((bf16[128,2688]{1,0:T(8,128)(2,1)}, bf16[128,2688]{1,0:T(8,128)(2,1)S(1)}, u32[]{:S(2)}) %copy-start) | copy-done | bytes 688152
  19.0 44.3 %shard_map.231 = (f32[640]{0:T(1024)}, f32[8,640]{1,0:T(8,128)}, f32[21,8,128]{2,1,0:T(8,128)}) custom-call(f32[144,640]{1,0:T(8,128)} %bitcast.14, s32[48,640]{1,0:T(8,128)} %bitcast.15, s32[640]{0:T(1024)} %count_ref.1, s32[640]{0:T(1024)} %species_ref.1, f32[100]{0:T(128)} %scale_ref.1, f32[100]{0:T(128)} %shift_ref.1, bf16[640,128]{1,0:T(8,128)(2,1)} %feat_ref.3, ...), custom_call_target="tpu_custom_call" | custom-call | flops 30000001024 | bytes 4000000 | tf_op jit(solution)/shard_map/pallas_call | solution.py:563
  63.3 0.9 %copy-done.2 = f32[21,8,128]{2,1,0:T(8,128)S(1)} copy-done((f32[21,8,128]{2,1,0:T(8,128)S(1)}, f32[21,8,128]{2,1,0:T(8,128)}, u32[]{:S(2)}) %copy-start.2) | copy-done | bytes 86040
  64.2 0.7 copy-done.5
  64.9 9.4 %shard_map.232 = f32[3,640]{1,0:T(4,128)S(1)} custom-call(f32[8,640]{1,0:T(8,128)S(1)} %copy-done.5, f32[21,8,128]{2,1,0:T(8,128)S(1)} %copy-done.2, s32[2,640]{1,0:T(2,128)S(1)} %bitcast.8, s32[2,256]{1,0:T(2,128)S(1)} %bitcast.10, s32[2,128]{1,0:T(2,128)S(1)} %bitcast.12, s32[1,6]{1,0:T(1,128)S(1)} %copy-done.8), custom_call_target="tpu_custom_call" | custom-call | tf_op jit(solution)/shard_map/pallas_call | solution.py:617
  74.3 0.6 copy.29
  (4 shorter events, 0.0 us)
Async XLA Ops:
  2.1 1.1 %copy-start.9 = (s32[30720]{0:T(1024)S(1)}, s32[30720]{0:T(1024)}, u32[]{:S(2)}) copy-start(s32[30720]{0:T(1024)} %param.25) | copy-start | bytes 368644
  3.4 0.9 %copy-start.1 = (bf16[640,128]{1,0:T(8,128)(2,1)S(1)}, bf16[640,128]{1,0:T(8,128)(2,1)}, u32[]{:S(2)}) copy-start(bf16[640,128]{1,0:T(8,128)(2,1)} %feat_ref.3) | copy-start | bytes 491524
  3.4 0.9 %copy-start.3 = (bf16[128,128]{1,0:T(8,128)(2,1)S(1)}, bf16[128,128]{1,0:T(8,128)(2,1)}, u32[]{:S(2)}) copy-start(bf16[128,128]{1,0:T(8,128)(2,1)} %w_ref.1) | copy-start | bytes 98308
  3.4 0.9 %copy-start.7 = (s32[1,2,128]{2,1,0:T(2,128)S(1)}, s32[1,2,128]{2,1,0:T(2,128)}, u32[]{:S(2)}) copy-start(s32[1,2,128]{2,1,0:T(2,128)} %param.30) | copy-start | bytes 3076
  4.2 0.7 copy-start.4
  4.2 0.7 copy-start.6
  4.2 0.7 copy-start.8
  18.1 0.8 %copy-start = (bf16[128,2688]{1,0:T(8,128)(2,1)}, bf16[128,2688]{1,0:T(8,128)(2,1)S(1)}, u32[]{:S(2)}) copy-start(bf16[128,2688]{1,0:T(8,128)(2,1)S(1)} %shard_map.230.table_ref) | copy-start | bytes 2064388
  63.3 0.9 %copy-start.2 = (f32[21,8,128]{2,1,0:T(8,128)S(1)}, f32[21,8,128]{2,1,0:T(8,128)}, u32[]{:S(2)}) copy-start(f32[21,8,128]{2,1,0:T(8,128)} %get-tuple-element.7.spread_ref) | copy-start | bytes 258052
  64.2 0.7 copy-start.5

commit v2 on v1

v2 whole, which is shorter than its diff:
```python
import math

import jax
import jax.numpy as jnp
from jax import lax
from jax.experimental import pallas as pl
from jax.experimental.pallas import tpu as pltpu
from jax.sharding import PartitionSpec as P

GAMMA = 10.0
CUTOFF = 5.0
LOG_TWO = math.log(2.0)
LOG2E = 1.0 / LOG_TWO
LANES = 128
UNROLL = 4
CHUNK = 256
RADIAL_ROWS = 64
GROUP_ROWS = 32
BEHIND = 2

BF16 = jnp.bfloat16
F32 = jnp.float32


def dot(a, b):
    return jnp.dot(a, b, preferred_element_type=F32)


def dot_nt(a, b):
    return lax.dot_general(a, b, (((1,), (1,)), ((), ())), preferred_element_type=F32)


def split3(value):
    high = value.astype(BF16)
    rest = value - high.astype(F32)
    middle = rest.astype(BF16)
    low = (rest - middle.astype(F32)).astype(BF16)
    return high, middle, low


def split2(value):
    high = value.astype(BF16)
    low = (value - high.astype(F32)).astype(BF16)
    return jnp.concatenate([high, low], axis=0)


def softplus_of(value):
    return jnp.maximum(value, 0.0) + jnp.log(1.0 + jnp.exp(-jnp.abs(value)))


def sigmoid_of(value):
    return 1.0 / (1.0 + jnp.exp(-value))


def one_hot(row, size):
    span = row.shape[1]
    parts = []
    for start in range(0, size, CHUNK):
        spot = jnp.broadcast_to(row - float(start), (16, span)).astype(BF16)
        lanes = lax.broadcasted_iota(jnp.int32, (16, span), 0).astype(F32)
        for b in range(min(CHUNK, size - start) // 16):
            ids = (lanes + float(16 * b)).astype(BF16)
            parts.append(jnp.where(ids == spot, jnp.ones((), BF16), jnp.zeros((), BF16)))
    return jnp.concatenate(parts, axis=0)


def flip(weight):
    return weight.astype(F32).T.astype(BF16)


def pair_kernel(
    rows_ref,
    order_ref,
    counts_ref,
    vals_ref,
    feat_ref,
    table_ref,
    square_ref,
    wide_ref,
    tall_ref,
    column_ref,
    energy_ref,
    own_ref,
    spread_ref,
    msg_ref,
    gm_ref,
    own3_ref,
    xj_ref,
    prod_ref,
    sig_ref,
    slope_ref,
    hid_a_ref,
    hid_b_ref,
    filt_a_ref,
    filt_b_ref,
    found_a_ref,
    found_b_ref,
    back_a_ref,
    back_b_ref,
    minus_a_ref,
    minus_b_ref,
    total_ref,
):
    width, atoms = feat_ref.shape
    tiles = atoms // LANES
    steps = (rows_ref.shape[1] - 1) // tiles
    span = UNROLL * LANES
    table_rows = table_ref.shape[1]
    idle = tiles * steps

    counts = counts_ref[0:1]
    scale = vals_ref[0:1]
    shift = vals_ref[8:9]
    feat = feat_ref[...].astype(F32)
    row_ref, dist_ref, env_ref, near_ref, far_ref = [rows_ref.at[n] for n in range(5)]

    w2, w2t, wo1, wo1t, wo2, wo2t = [square_ref[n] for n in range(6)]
    w1_back, we1 = wide_ref[0], wide_ref[1]
    w1t, we1t = tall_ref[0], tall_ref[1]
    b_f2, b_o1, b_o2, mu, sharp = [column_ref[:, n : n + 1] for n in range(5)]
    mu, sharp = mu[0:RADIAL_ROWS], sharp[0:RADIAL_ROWS]
    b_e1, w_e2 = [column_ref[0 : we1.shape[0], n : n + 1] for n in (5, 6)]

    def lane_row(ref, at):
        return jnp.concatenate([ref[at, u : u + 1, :] for u in range(UNROLL)], axis=1)

    ends = []
    items = jnp.zeros((), jnp.int32)
    for tile in range(tiles):
        most = jnp.max(counts[:, tile * LANES : (tile + 1) * LANES]).astype(jnp.int32)
        items = items + (most + (UNROLL - 1)) // UNROLL
        ends.append(items)
    rounds = (items + 1) // 2
    turns = (items + 3) // 4

    def place(item):
        tile = jnp.zeros((), jnp.int32)
        first = jnp.zeros((), jnp.int32)
        for end in ends[:-1]:
            past = item >= end
            tile = tile + past.astype(jnp.int32)
            first = jnp.where(past, end, first)
        at = jnp.where((item >= 0) & (item < items), tile * steps + item - first, idle)
        return tile, at

    def gather(row):
        return dot(table_ref[...], one_hot(row, table_rows))

    def radial_dot(at):
        offset = lane_row(dist_ref, at) - mu
        basis = jnp.exp2(sharp * (offset * offset))
        return (offset * basis).astype(BF16), dot(w1t, basis.astype(BF16))

    def activate(pre):
        grown = jnp.exp2(pre * LOG2E)
        total = 1.0 + grown
        sig = (grown * pl.reciprocal(total, approx=True)).astype(BF16)
        return sig, (jnp.log2(total) - 1.0).astype(BF16)

    def begin(item, hid_ref):
        slope, pre = radial_dot(place(item)[1])
        slope_ref[item + BEHIND] = slope
        sig, hidden = activate(pre)
        sig_ref[item + BEHIND] = sig
        hid_ref[...] = hidden

    def finish(item, filt_ref, found_ref):
        tile, at = place(item)
        prod = found_ref[...] * filt_ref[...]
        prod_ref[item + BEHIND] = prod.astype(BF16)
        weighted = prod * lane_row(env_ref, at)
        part = msg_ref[tile]
        for u in range(UNROLL):
            part = part + weighted[:, u * LANES : (u + 1) * LANES]
        msg_ref[tile] = part

    def forward(item, hid_ref, next_ref, filt_ref, found_ref, last_filt_ref, last_found_ref):
        filt = dot(w2t, hid_ref[...]) + b_f2
        slope, pre = radial_dot(place(item + 1)[1])
        slope_ref[item + BEHIND + 1] = slope
        found = gather(lane_row(row_ref, place(item)[1]))
        sig, hidden = activate(pre)
        sig_ref[item + BEHIND + 1] = sig
        next_ref[...] = hidden
        finish(item - 1, last_filt_ref, last_found_ref)
        filt_ref[...] = filt
        found_ref[...] = found
        xj_ref[item + BEHIND] = found.astype(BF16)

    msg_ref[...] = jnp.zeros_like(msg_ref)
    filt_b_ref[...] = jnp.zeros_like(filt_b_ref)
    found_b_ref[...] = jnp.zeros_like(found_b_ref)
    begin(jnp.zeros((), jnp.int32), hid_a_ref)

    def forward_round(turn, carry):
        item = 4 * turn
        forward(item, hid_a_ref, hid_b_ref, filt_a_ref, found_a_ref, filt_b_ref, found_b_ref)
        forward(item + 1, hid_b_ref, hid_a_ref, filt_b_ref, found_b_ref, filt_a_ref, found_a_ref)
        forward(item + 2, hid_a_ref, hid_b_ref, filt_a_ref, found_a_ref, filt_b_ref, found_b_ref)
        forward(item + 3, hid_b_ref, hid_a_ref, filt_b_ref, found_b_ref, filt_a_ref, found_a_ref)
        return carry

    lax.fori_loop(0, turns, forward_round, 0)
    finish(4 * turns - 1, filt_b_ref, found_b_ref)

    message = jnp.concatenate([msg_ref[t] for t in range(tiles)], axis=1)
    message = (message * LOG_TWO).astype(BF16)
    out_pre = dot(wo1t, message) + b_o1
    out_mid = (softplus_of(out_pre) - LOG_TWO).astype(BF16)
    updated = (feat + dot(wo2t, out_mid) + b_o2).astype(BF16)
    energy_pre = dot(we1, updated) + b_e1
    soft = softplus_of(energy_pre) - LOG_TWO
    energy = scale * jnp.sum(soft * w_e2, axis=0, keepdims=True) + shift
    home = one_hot(order_ref[0:1], atoms)
    plain = dot(split2(jnp.broadcast_to(energy, (8, atoms))), home)
    energy_ref[...] = (plain[0:1] + plain[8:9]).reshape(atoms)
    grad_head = (scale * w_e2 * sigmoid_of(energy_pre)).astype(BF16)
    grad_update = dot(we1t, grad_head).astype(BF16)
    grad_mid = (dot(wo2, grad_update) * sigmoid_of(out_pre)).astype(BF16)
    grad_message = dot(wo1, grad_mid)
    for tile in range(tiles):
        gm_ref[tile] = grad_message[:, tile * LANES : (tile + 1) * LANES]

    total_ref[...] = jnp.zeros_like(total_ref)
    own3_ref[...] = jnp.zeros_like(own3_ref)
    for ref in (back_a_ref, back_b_ref, minus_a_ref, minus_b_ref):
        ref[...] = jnp.zeros_like(ref)
    for early in range(BEHIND):
        prod_ref[early] = jnp.zeros((width, span), BF16)
        slope_ref[early] = jnp.zeros((RADIAL_ROWS, span), BF16)
    for late in range(4):
        ahead = 2 * rounds + BEHIND + late
        xj_ref[ahead] = jnp.zeros((width, span), BF16)
        prod_ref[ahead] = jnp.zeros((width, span), BF16)
        slope_ref[ahead] = jnp.zeros((RADIAL_ROWS, span), BF16)
        sig_ref[ahead] = jnp.zeros((width, span), BF16)

    def pull(item):
        tile, at = place(item)
        grad_b = gm_ref[tile].astype(BF16)
        grad_b_wide = jnp.concatenate([grad_b] * UNROLL, axis=1)
        mixed = dot(w2, grad_b_wide * xj_ref[item + BEHIND])
        return (mixed * sig_ref[item + BEHIND].astype(F32)).astype(BF16)

    def settle(item, grad_pre):
        tile, at = place(item)
        grad_basis = dot(w1_back, grad_pre)
        grad_wide = jnp.concatenate([gm_ref[tile]] * UNROLL, axis=1)
        s1 = jnp.sum(grad_basis * slope_ref[item + BEHIND].astype(F32), axis=0, keepdims=True)
        s2 = jnp.sum(grad_wide * prod_ref[item + BEHIND].astype(F32), axis=0, keepdims=True)
        ratio = s1 * lane_row(near_ref, at) + s2 * lane_row(far_ref, at)
        forces = []
        for c in range(3):
            force = ratio * lane_row(rows_ref.at[5 + c], at)
            part = own3_ref[tile, c : c + 1, :]
            for u in range(UNROLL):
                part = part + force[:, u * LANES : (u + 1) * LANES]
            own3_ref[tile, c : c + 1, :] = part
            forces.append(-force)
        return jnp.concatenate(forces, axis=0)

    def strew(item, minus):
        row = lane_row(row_ref, place(item)[1])
        high = jnp.floor(row * (1.0 / 128))
        low = row - high * 128.0
        wide = (16, span)
        high_b = jnp.broadcast_to(high, wide).astype(BF16)
        low_b = jnp.broadcast_to(low, wide).astype(BF16)
        lanes = lax.broadcasted_iota(jnp.int32, wide, 0).astype(F32)
        ids = [(lanes + float(16 * b)).astype(BF16) for b in range(8)]
        lower = jnp.concatenate(
            [jnp.where(one == low_b, jnp.ones((), BF16), jnp.zeros((), BF16)) for one in ids],
            axis=0,
        )
        here = [ids[b] == high_b for b in range(GROUP_ROWS // 16)]
        placed = []
        for c in range(3):
            part = jnp.broadcast_to(minus[c : c + 1], wide).astype(BF16)
            placed += [jnp.where(mask, part, jnp.zeros((), BF16)) for mask in here]
        return dot_nt(jnp.concatenate(placed, axis=0), lower)

    def backward_round(turn, carry):
        item = 2 * turn
        spread_a = strew(item - 4, minus_a_ref[0:3])
        spread_b = strew(item - 3, minus_b_ref[0:3])
        minus_a = settle(item - 2, back_a_ref[...])
        minus_b = settle(item - 1, back_b_ref[...])
        pull_a = pull(item)
        pull_b = pull(item + 1)
        total_ref[...] = total_ref[...] + spread_a + spread_b
        minus_a_ref[0:3] = minus_a
        minus_b_ref[0:3] = minus_b
        back_a_ref[...] = pull_a
        back_b_ref[...] = pull_b
        return carry

    lax.fori_loop(0, rounds + 2, backward_round, 0)

    for tile in range(tiles):
        own_ref[:, tile * LANES : (tile + 1) * LANES] = own3_ref[tile]
    spread_ref[...] = jnp.zeros_like(spread_ref)
    for c in range(3):
        spread_ref[:, c, :] = total_ref[c * GROUP_ROWS : c * GROUP_ROWS + spread_ref.shape[0]]


def neighbours():
    found = []
    for axis in ("gx", "gy", "gz"):
        size = lax.axis_size(axis)
        place = lax.axis_index(axis)
        found.append({axis: lax.rem(place + 1, size)})
        found.append({axis: lax.rem(place + size - 1, size)})
    return found


def greet(found):
    barrier = pltpu.get_barrier_semaphore()
    for device in found:
        pl.semaphore_signal(
            barrier, inc=1, device_id=device, device_id_type=pl.DeviceIdType.MESH
        )
    pl.semaphore_wait(barrier, len(found))


FACES = ((0, 1, 1, 0), (0, 0, 0, 1), (1, 1, 3, 2), (1, 0, 2, 3), (2, 1, 5, 4), (2, 0, 4, 5))


def ready_weights(
    w1_ref,
    b1_ref,
    w2_ref,
    wo1_ref,
    wo2_ref,
    we1_ref,
    bf2_ref,
    bo1_ref,
    bo2_ref,
    be1_ref,
    w_e2_ref,
    square_ref,
    wide_ref,
    tall_ref,
    column_ref,
):
    radial, width = w1_ref.shape
    bias = b1_ref[...].reshape(1, width)
    bias_high = bias.astype(BF16).astype(F32)
    bias_middle = (bias - bias_high).astype(BF16).astype(F32)
    w1 = jnp.concatenate(
        [
            w1_ref[...].astype(F32),
            bias_high,
            bias_middle,
            bias - bias_high - bias_middle,
            jnp.zeros((RADIAL_ROWS - radial - 3, width), F32),
        ],
        axis=0,
    )
    radial_col = lax.broadcasted_iota(jnp.int32, (RADIAL_ROWS, 1), 0)
    tall_ref[0] = w1.T.astype(BF16)
    wide_ref[0] = jnp.where(radial_col < radial, w1, 0.0).astype(BF16)
    wide_ref[1] = we1_ref[...]
    tall_ref[1] = flip(we1_ref[...])
    for n, ref in enumerate((w2_ref, wo1_ref, wo2_ref)):
        square_ref[2 * n] = ref[...]
        square_ref[2 * n + 1] = flip(ref[...])
    ids = lax.broadcasted_iota(jnp.int32, (1, width), 1)
    rows = [
        bf2_ref[...].reshape(1, width) * LOG2E,
        bo1_ref[...].reshape(1, width),
        bo2_ref[...].reshape(1, width),
        ids.astype(F32) * (CUTOFF / (radial - 1)),
        jnp.where(ids < radial, -GAMMA * LOG2E, 0.0),
    ]
    for ref in (be1_ref, w_e2_ref):
        size = ref.shape[0]
        rows.append(
            jnp.concatenate(
                [ref[...].reshape(1, size), jnp.zeros((1, width - size), F32)], axis=1
            )
        )
    rows.append(jnp.zeros((width - len(rows), width), F32))
    column_ref[...] = jnp.concatenate(rows, axis=0).T


def prepare(
    feat_ref,
    disp_ref,
    index_ref,
    count_ref,
    species_ref,
    scale_ref,
    shift_ref,
    rows_ref,
    order_ref,
    counts_ref,
    vals_ref,
    sorted_ref,
    raw_ref,
    rank_ref,
):
    atoms = feat_ref.shape[0]
    slots = disp_ref.shape[1] // atoms
    tiles = atoms // LANES
    steps = slots // UNROLL
    idle = tiles * steps
    block = math.lcm(slots, LANES)
    lines = block // LANES
    each = block // slots
    groups = atoms // each

    raw_ref[...] = jnp.zeros_like(raw_ref)

    def lay(g, carry):
        for m in range(lines):
            at = pl.multiple_of((g * lines + m) * LANES, LANES)
            three = disp_ref[:, pl.ds(at, LANES)]
            for c in range(3):
                raw_ref[c, m, pl.ds(g, 1), :] = three[c : c + 1]
            line = index_ref[pl.ds(g * lines + m, 1), :]
            raw_ref[3, m, pl.ds(g, 1), :] = line.astype(F32)
        return carry

    lax.fori_loop(0, groups, lay, 0)

    atom_row = lax.broadcasted_iota(jnp.int32, (1, atoms), 1)
    atom_col = lax.broadcasted_iota(jnp.int32, (atoms, 1), 0)
    count_row = count_ref[...].reshape(1, atoms)
    key_row = (count_row * atoms - atom_row).astype(F32)
    count_col = jnp.broadcast_to(count_row.astype(F32), (128, atoms)).T[:, 0:1]
    key_col = count_col * float(atoms) - atom_col.astype(F32)
    rank_col = jnp.sum(jnp.where(key_row > key_col, 1.0, 0.0), axis=1, keepdims=True)
    perm = jnp.where(rank_col == atom_row.astype(F32), 1.0, 0.0).astype(BF16)

    rank_ref[...] = jnp.broadcast_to(rank_col, (atoms, LANES))
    order_ref[...] = rank_ref[...].T[0:8]
    lane_ids = lax.broadcasted_iota(jnp.int32, (groups, LANES), 1).astype(F32)
    blocks = []
    for a in range(each):
        rank = rank_ref[pl.ds(a, groups, stride=each), :]
        blocks.append(
            jnp.concatenate(
                [
                    jnp.where(rank - float(t * LANES) == lane_ids, 1.0, 0.0).astype(BF16)
                    for t in range(tiles)
                ],
                axis=1,
            )
        )
        if groups < LANES:
            blocks.append(jnp.zeros((LANES - groups, atoms), BF16))
    spots = jnp.concatenate(blocks, axis=0)

    def columns(c):
        turned = jnp.concatenate([raw_ref[c, m].T for m in range(lines)], axis=0)
        return jnp.concatenate(
            [turned[a * slots : (a + 1) * slots] for a in range(each)], axis=1
        )

    def put(ref, value):
        for tile in range(tiles):
            for s in range(steps):
                ref[tile * steps + s] = value[
                    s * UNROLL : (s + 1) * UNROLL, tile * LANES : (tile + 1) * LANES
                ]
        ref[idle] = jnp.zeros((UNROLL, LANES), F32)

    raw = jnp.concatenate([columns(c) for c in range(3)], axis=0)
    index = columns(3)
    index_high = jnp.floor(index * (1.0 / 128))
    index_low = index - index_high * 128.0
    stack = jnp.concatenate(
        list(split3(raw)) + [index_high.astype(BF16), index_low.astype(BF16)], axis=0
    )
    found = dot(stack, spots)
    size = 3 * slots
    disp = found[0:size] + found[size : 2 * size] + found[2 * size : 3 * size]
    put(
        rows_ref.at[0],
        found[3 * size : 3 * size + slots] * 128.0 + found[3 * size + slots : 3 * size + 2 * slots],
    )
    counts8 = dot(jnp.broadcast_to(count_row, (8, atoms)).astype(F32).astype(BF16), perm)
    counts = counts8[0:1]
    counts_ref[...] = counts8
    kinds = scale_ref.shape[0]
    kind_ids = lax.broadcasted_iota(jnp.int32, (kinds, 1), 0)
    kind_pick = jnp.where(kind_ids == species_ref[...].reshape(1, atoms), 1.0, 0.0).astype(BF16)
    pair_of = jnp.concatenate(
        [
            jnp.broadcast_to(scale_ref[...].reshape(1, kinds), (8, kinds)),
            jnp.broadcast_to(shift_ref[...].reshape(1, kinds), (8, kinds)),
        ],
        axis=0,
    )
    atom_vals = sum(dot(part, kind_pick) for part in split3(pair_of))
    vals_ref[...] = sum(dot(part, perm) for part in split3(atom_vals))
    sorted_ref[...] = dot(feat_ref[...].astype(F32).T.astype(BF16), perm).astype(BF16)

    dx = disp[0:slots]
    dy = disp[slots : 2 * slots]
    dz = disp[2 * slots : 3 * slots]
    squared = dx * dx + dy * dy + dz * dz
    distance = jnp.sqrt(squared)
    put(rows_ref.at[1], distance)
    slot_ids = lax.broadcasted_iota(jnp.int32, (slots, 1), 0).astype(F32)
    live = jnp.where(slot_ids < counts, 1.0, 0.0)
    y = (math.pi / CUTOFF) * distance - 0.5 * math.pi
    y2 = y * y
    sin_y = y * (
        1.0
        + y2
        * (
            -1.0 / 6
            + y2 * (1.0 / 120 + y2 * (-1.0 / 5040 + y2 * (1.0 / 362880 - y2 * (1.0 / 39916800))))
        )
    )
    envelope = (0.5 - 0.5 * sin_y) * live
    put(rows_ref.at[2], envelope)
    cos_y = 1.0 + y2 * (
        -0.5
        + y2
        * (
            1.0 / 24
            + y2
            * (
                -1.0 / 720
                + y2 * (1.0 / 40320 + y2 * (-1.0 / 3628800 + y2 * (1.0 / 479001600)))
            )
        )
    )
    inverse = live / distance
    put(rows_ref.at[3], envelope * (-2.0 * GAMMA) * inverse)
    put(rows_ref.at[4], (-0.5 * math.pi / CUTOFF * LOG_TWO) * cos_y * inverse)
    put(rows_ref.at[5], dx)
    put(rows_ref.at[6], dy)
    put(rows_ref.at[7], dz)


INPUTS = 23
OUTPUTS = 9


def named_faces(lists, used_ref):
    found = []
    used = used_ref[...]
    for dim, side, column, _ in FACES:
        names = lists[dim][side : side + 1, :]
        lanes = lax.broadcasted_iota(jnp.int32, names.shape, 1)
        found.append(jnp.where(lanes < used[:, column : column + 1], names, -1).astype(F32))
    return found


def send_kernel(*refs):
    far, refs = refs[:INPUTS], refs[INPUTS:]
    table_ref, results, refs = refs[0], refs[1 : OUTPUTS + 1], refs[OUTPUTS + 1 :]
    near, made, refs = refs[:INPUTS], refs[INPUTS : INPUTS + OUTPUTS], refs[INPUTS + OUTPUTS :]
    mine_ref, stage_ref, raw_ref, rank_ref, load_sem, save_sem, send_sem, recv_sem = refs
    loads = [
        pltpu.make_async_copy(one, two, load_sem.at[n])
        for n, (one, two) in enumerate(zip(far, near))
    ]
    for load in loads:
        load.start()
    found = neighbours()
    greet(found)
    feat_ref, w_ref = near[0:2]
    atoms = feat_ref.shape[0]
    for load in loads[0:6]:
        load.wait()
    x_t = dot(feat_ref[...], w_ref[...]).T.astype(BF16)
    copies = []
    start = 0
    for n, names in enumerate(named_faces(near[2:5], near[5])):
        length = names.shape[1]
        stage_ref[:, start : start + length] = dot(x_t, one_hot(names, atoms)).astype(BF16)
        copy = pltpu.make_async_remote_copy(
            src_ref=stage_ref.at[:, pl.ds(start, length)],
            dst_ref=table_ref.at[:, pl.ds(atoms + start, length)],
            send_sem=send_sem.at[n],
            recv_sem=recv_sem.at[n],
            device_id=found[n],
            device_id_type=pl.DeviceIdType.MESH,
        )
        copy.start()
        copies.append(copy)
        start += length
    mine_ref[...] = x_t
    saves = [pltpu.make_async_copy(mine_ref, table_ref.at[:, pl.ds(0, atoms)], save_sem.at[0])]
    saves[0].start()
    for load in loads[6:]:
        load.wait()
    rows_ref, order_ref, counts_ref, vals_ref, sorted_ref = made[0:5]
    prepare(
        feat_ref,
        *near[6:12],
        rows_ref,
        order_ref,
        counts_ref,
        vals_ref,
        sorted_ref,
        raw_ref,
        rank_ref,
    )
    ready_weights(*near[12:], *made[5:])
    for n, (one, two) in enumerate(zip(made, results)):
        save = pltpu.make_async_copy(one, two, save_sem.at[n + 1])
        save.start()
        saves.append(save)
    for copy in saves + copies:
        copy.wait()


def return_kernel(
    own_ref,
    spread_ref,
    order_ref,
    ex_ref,
    ey_ref,
    ez_ref,
    used_ref,
    force_ref,
    own_here,
    order_here,
    ex_here,
    ey_here,
    ez_here,
    used_here,
    mine_ref,
    land_ref,
    load_sem,
    send_sem,
    recv_sem,
):
    atoms = force_ref.shape[1]
    group = atoms // 128
    pairs = (
        (spread_ref.at[pl.ds(0, group)], mine_ref),
        (own_ref, own_here),
        (order_ref, order_here),
        (ex_ref, ex_here),
        (ey_ref, ey_here),
        (ez_ref, ez_here),
        (used_ref, used_here),
    )
    loads = [
        pltpu.make_async_copy(one, two, load_sem.at[n]) for n, (one, two) in enumerate(pairs)
    ]
    for load in loads:
        load.start()
    lists = (ex_here, ey_here, ez_here)
    found = neighbours()
    greet(found)
    copies = []
    start = 0
    for n, (dim, _, _, to) in enumerate(FACES):
        length = lists[dim].shape[1] // 128
        copy = pltpu.make_async_remote_copy(
            src_ref=spread_ref.at[pl.ds(group + start, length)],
            dst_ref=land_ref.at[pl.ds(start, length)],
            send_sem=send_sem.at[n],
            recv_sem=recv_sem.at[n],
            device_id=found[to ^ 1],
            device_id_type=pl.DeviceIdType.MESH,
        )
        copy.start()
        copies.append(copy)
        start += length
    for load in loads:
        load.wait()
    picks = jnp.concatenate(
        [one_hot(names, atoms) for names in named_faces(lists, used_here)], axis=1
    )
    total = jnp.concatenate([mine_ref[h] for h in range(group)], axis=1)
    part = dot(split2(own_here[...]), one_hot(order_here[0:1], atoms))
    total = total + part[0:8] + part[8:16]
    for copy in copies:
        copy.wait()
    values = jnp.concatenate([land_ref[h] for h in range(start)], axis=1)
    part = dot_nt(split2(values), picks)
    total = total + part[0:8] + part[8:16]
    force_ref[...] = total[0:3]


def body(
    features,
    displacement,
    neighbour,
    neighbour_count,
    species,
    exports_x,
    exports_y,
    exports_z,
    face_counts,
    w_in,
    w_f1,
    b_f1,
    w_f2,
    b_f2,
    w_o1,
    b_o1,
    w_o2,
    b_o2,
    w_e1,
    b_e1,
    w_e2,
    species_scale,
    species_shift,
):
    atom_rows, width = features.shape
    slot_count = neighbour.shape[0] // atom_rows
    vmem = pl.BlockSpec(memory_space=pltpu.VMEM)
    lists = (exports_x[0], exports_y[0], exports_z[0])
    ghost_rows = sum(2 * one.shape[1] for one in lists)
    table_rows = atom_rows + ghost_rows
    tiles = atom_rows // LANES
    steps = slot_count // UNROLL * tiles
    groups = table_rows // 128
    lines = math.lcm(slot_count, LANES) // LANES
    inputs = (
        features,
        w_in,
        *lists,
        face_counts,
        displacement,
        neighbour.reshape(-1, LANES),
        neighbour_count,
        species,
        species_scale,
        species_shift,
        w_f1,
        b_f1,
        w_f2,
        w_o1,
        w_o2,
        w_e1.T,
        b_f2,
        b_o1,
        b_o2,
        b_e1,
        w_e2,
    )
    hidden = w_e1.shape[1]
    anywhere = pl.BlockSpec(memory_space=pl.ANY)
    results = (
        jax.ShapeDtypeStruct((8, steps + 1, UNROLL, LANES), F32),
        jax.ShapeDtypeStruct((8, atom_rows), F32),
        jax.ShapeDtypeStruct((8, atom_rows), F32),
        jax.ShapeDtypeStruct((16, atom_rows), F32),
        jax.ShapeDtypeStruct((width, atom_rows), BF16),
        jax.ShapeDtypeStruct((6, width, width), BF16),
        jax.ShapeDtypeStruct((2, hidden, width), BF16),
        jax.ShapeDtypeStruct((2, width, hidden), BF16),
        jax.ShapeDtypeStruct((width, width), F32),
    )
    table_t, rows, order, counts, vals, sorted_t, *weights = pl.pallas_call(
        send_kernel,
        out_shape=(jax.ShapeDtypeStruct((width, table_rows), BF16),) + results,
        in_specs=[anywhere] * len(inputs),
        out_specs=(anywhere,) * (1 + len(results)),
        scratch_shapes=[pltpu.VMEM(one.shape, one.dtype) for one in inputs + results]
        + [
            pltpu.VMEM((width, atom_rows), BF16),
            pltpu.VMEM((width, ghost_rows), BF16),
            pltpu.VMEM((4, lines, LANES, LANES), F32),
            pltpu.VMEM((atom_rows, LANES), F32),
            pltpu.SemaphoreType.DMA((len(inputs),)),
            pltpu.SemaphoreType.DMA((1 + len(results),)),
            pltpu.SemaphoreType.DMA((6,)),
            pltpu.SemaphoreType.DMA((6,)),
        ],
        compiler_params=pltpu.CompilerParams(
            collective_id=0, has_side_effects=True, vmem_limit_bytes=58 * 1024 * 1024
        ),
    )(*inputs)
    span = UNROLL * LANES
    energy, own_force, spread = pl.pallas_call(
        pair_kernel,
        out_shape=(
            jax.ShapeDtypeStruct((atom_rows,), F32),
            jax.ShapeDtypeStruct((8, atom_rows), F32),
            jax.ShapeDtypeStruct((groups, 8, 128), F32),
        ),
        in_specs=[vmem] * 10,
        out_specs=(vmem, vmem, vmem),
        scratch_shapes=[
            pltpu.VMEM((tiles, width, LANES), F32),
            pltpu.VMEM((tiles, width, LANES), F32),
            pltpu.VMEM((tiles, 8, LANES), F32),
            pltpu.VMEM((steps + 10, width, span), BF16),
            pltpu.VMEM((steps + 10, width, span), BF16),
            pltpu.VMEM((steps + 10, width, span), BF16),
            pltpu.VMEM((steps + 10, RADIAL_ROWS, span), BF16),
            pltpu.VMEM((width, span), BF16),
            pltpu.VMEM((width, span), BF16),
            pltpu.VMEM((width, span), F32),
            pltpu.VMEM((width, span), F32),
            pltpu.VMEM((width, span), F32),
            pltpu.VMEM((width, span), F32),
            pltpu.VMEM((width, span), BF16),
            pltpu.VMEM((width, span), BF16),
            pltpu.VMEM((8, span), F32),
            pltpu.VMEM((8, span), F32),
            pltpu.VMEM((3 * GROUP_ROWS, 128), F32),
        ],
        compiler_params=pltpu.CompilerParams(vmem_limit_bytes=58 * 1024 * 1024),
        cost_estimate=pl.CostEstimate(
            flops=30_000_000_000, bytes_accessed=4_000_000, transcendentals=16_000_000
        ),
    )(
        rows,
        order,
        counts,
        vals,
        sorted_t,
        table_t,
        *weights,
    )
    last = (own_force, spread, order, *lists, face_counts)
    copied = (own_force, order, *lists, face_counts)
    forces = pl.pallas_call(
        return_kernel,
        out_shape=jax.ShapeDtypeStruct((3, atom_rows), F32),
        in_specs=[anywhere] * len(last),
        out_specs=vmem,
        scratch_shapes=[pltpu.VMEM(one.shape, one.dtype) for one in copied]
        + [
            pltpu.VMEM((tiles, 8, LANES), F32),
            pltpu.VMEM((ghost_rows // 128, 8, 128), F32),
            pltpu.SemaphoreType.DMA((len(last),)),
            pltpu.SemaphoreType.DMA((6,)),
            pltpu.SemaphoreType.DMA((6,)),
        ],
        compiler_params=pltpu.CompilerParams(
            collective_id=1, has_side_effects=True, vmem_limit_bytes=58 * 1024 * 1024
        ),
    )(*last)
    return (energy, forces)


def solution(mesh):
    both = ("geom", "gx", "gy", "gz")
    return jax.shard_map(
        body,
        mesh=mesh,
        in_specs=(
            P(both, None),
            P(None, both),
            P(both),
            P(both),
            P(both),
            P(both, None, None),
            P(both, None, None),
            P(both, None, None),
            P(both, None),
        )
        + (P(),) * 14,
        out_specs=(P(both), P(None, both)),
        check_vma=False,
    )
```

time: 75.3 us -> 61 us (0.81)
  Pallas kernels: 66.9 us -> 58.6 us
  local copies, waits for them, and re-layouts: 7.29 us -> 1.3 us
    pallas_call x1, Pallas kernels: 44.3 us -> 36.2 us  [body(): pl.pallas_call(pair_kernel, out_shape=(jax.ShapeDtypeStruct((atom_rows,),...]
    unnamed x21 -> x1, local copies, waits for them, and re-layouts: 3.79 us -> 1.3 us
    reshape x3 -> x0, local copies, waits for them, and re-layouts: 2.44 us -> none  [the longest x1 1.51 us: body(): displacement.reshape(3, atom_rows, slot_count).transpose(0, 2, 1)]
    transpose x1 -> x0, local copies, waits for them, and re-layouts: 1.06 us -> none  [body(): displacement.reshape(3, atom_rows, slot_count).transpose(0, 2, 1)]
where the time goes in v2:
time: 61 us; the launch traced here: 60.6 us
  Pallas kernels  58.6 us (96%)
  local copies, waits for them, and re-layouts  1.3 us (2%)
  between operations  0.65 us (1%)
    pallas_call x1, Pallas kernels, body(): pl.pallas_call(pair_kernel, out_shape=(jax.ShapeDtypeStruct((atom_rows,),...  36.2 us
    pallas_call x1, Pallas kernels, body(): pl.pallas_call(send_kernel, out_shape=(jax.ShapeDtypeStruct((width, table...  13.4 us
    pallas_call x1, Pallas kernels, body(): pl.pallas_call(return_kernel, out_shape=jax.ShapeDtypeStruct((3, atom_row...  9.07 us
    unnamed x1, local copies, waits for them, and re-layouts  1.3 us

profile of v2, /device:TPU:0, one launch (start us, length us, event | category | flops | bytes accessed | tf_op | source)
XLA Modules:
  0.0 60.6 jit_solution(8920239319081874002)
XLA Ops:
  0.6 13.4 %shard_map.230 = (bf16[128,2688]{1,0:T(8,128)(2,1)}, f32[8,61,4,128]{3,2,1,0:T(4,128)}, f32[8,640]{1,0:T(8,128)}, f32[8,640]{1,0:T(8,128)}, f32[16,640]{1,0:T(8,...) custom-call(bf16[640,128]{1,0:T(8,128)(2,1)} %refs_0_.1, ...), custom_call_target="tpu_custom_call" | custom-call | tf_op jit(solution)/shard_map/pallas_call | solution.py:755
  14.0 36.2 %shard_map.231 = (f32[640]{0:T(1024)}, f32[8,640]{1,0:T(8,128)}, f32[21,8,128]{2,1,0:T(8,128)}) custom-call(f32[8,61,4,128]{3,2,1,0:T(4,128)} %get-tuple-element.15.rows_ref, f32[8,640]{1,0:T(8,128)} %get-tuple-element.16.order_ref, f32[8,640]{1,0:T(8,128)} %get-tuple-element.17.counts_ref, f32[16,640]{1,0:T(8,128)} %get-tuple-element.18.vals_ref, ...), custom_call_target="tpu_custom_call" | custom-call | flops 30000001024 | bytes 4000000 | tf_op jit(solution)/shard_map/pallas_call | solution.py:776
  50.2 9.1 %shard_map.232 = f32[3,640]{1,0:T(4,128)} custom-call(f32[8,640]{1,0:T(8,128)} %get-tuple-element.26.own_ref, f32[21,8,128]{2,1,0:T(8,128)} %get-tuple-element.27.spread_ref, f32[8,640]{1,0:T(8,128)} %get-tuple-element.16.order_ref, s32[2,640]{1,0:T(2,128)} %bitcast.7, s32[2,256]{1,0:T(2,128)} %bitcast.10, s32[2,128]{1,0:T(2,128)} %bitcast.12, s32[1,6]{1,0:T(1,128)} %used_ref.1), custom_call_target="tpu_custom_call" | custom-call | tf_op jit(solution)/shard_map/pallas_call | solution.py:820
  59.3 1.3 %copy.26 = f32[3,640]{1,0:T(4,128)} copy(f32[3,640]{1,0:T(4,128)} %shard_map.232) | data formatting | bytes 15360

commit v3 on v2

--- a/solution.py
+++ b/solution.py
@@ -1,3 +1,4 @@
+import functools
 import math
 
 import jax
@@ -69,6 +70,7 @@
 
 
 def pair_kernel(
+    lengths,
     rows_ref,
     order_ref,
     counts_ref,
@@ -79,6 +81,7 @@
     wide_ref,
     tall_ref,
     column_ref,
+    held_ref,
     energy_ref,
     own_ref,
     spread_ref,
@@ -100,6 +103,7 @@
     minus_a_ref,
     minus_b_ref,
     total_ref,
+    packed_ref,
 ):
     width, atoms = feat_ref.shape
     tiles = atoms // LANES
@@ -143,8 +147,27 @@
         at = jnp.where((item >= 0) & (item < items), tile * steps + item - first, idle)
         return tile, at
 
-    def gather(row):
-        return dot(table_ref[...], one_hot(row, table_rows))
+    packed_ref[...] = jnp.zeros_like(packed_ref)
+    packed_ref[:, 0:atoms] = table_ref[:, 0:atoms]
+    lane_ids = lax.broadcasted_iota(jnp.int32, (width, LANES), 1)
+    packed_rows = jnp.full((), atoms, jnp.int32)
+    edge = atoms
+    for n, length in enumerate(lengths):
+        turn = packed_rows & (LANES - 1)
+        base = packed_rows - turn
+        below = lane_ids < turn
+        first = pl.multiple_of(base, LANES)
+        last = packed_ref[:, pl.ds(first, LANES)].astype(F32)
+        for t in range(length // LANES):
+            slab = table_ref[:, edge + t * LANES : edge + (t + 1) * LANES].astype(F32)
+            slab = pltpu.roll(slab, turn, 1)
+            at = pl.multiple_of(base + t * LANES, LANES)
+            packed_ref[:, pl.ds(at, LANES)] = jnp.where(below, last, slab).astype(BF16)
+            last = slab
+        at = pl.multiple_of(base + length, LANES)
+        packed_ref[:, pl.ds(at, LANES)] = jnp.where(below, last, 0.0).astype(BF16)
+        packed_rows = packed_rows + held_ref[n, 0]
+        edge += length
 
     def radial_dot(at):
         offset = lane_row(dist_ref, at) - mu
@@ -174,11 +197,12 @@
             part = part + weighted[:, u * LANES : (u + 1) * LANES]
         msg_ref[tile] = part
 
-    def forward(item, hid_ref, next_ref, filt_ref, found_ref, last_filt_ref, last_found_ref):
+    def forward(size, item, hid_ref, next_ref, filt_ref, found_ref, last_filt_ref, last_found_ref):
         filt = dot(w2t, hid_ref[...]) + b_f2
         slope, pre = radial_dot(place(item + 1)[1])
         slope_ref[item + BEHIND + 1] = slope
-        found = gather(lane_row(row_ref, place(item)[1]))
+        picked = one_hot(lane_row(rows_ref.at[8], place(item)[1]), size)
+        found = dot(packed_ref[:, 0:size], picked)
         sig, hidden = activate(pre)
         sig_ref[item + BEHIND + 1] = sig
         next_ref[...] = hidden
@@ -192,15 +216,29 @@
     found_b_ref[...] = jnp.zeros_like(found_b_ref)
     begin(jnp.zeros((), jnp.int32), hid_a_ref)
 
-    def forward_round(turn, carry):
-        item = 4 * turn
-        forward(item, hid_a_ref, hid_b_ref, filt_a_ref, found_a_ref, filt_b_ref, found_b_ref)
-        forward(item + 1, hid_b_ref, hid_a_ref, filt_b_ref, found_b_ref, filt_a_ref, found_a_ref)
-        forward(item + 2, hid_a_ref, hid_b_ref, filt_a_ref, found_a_ref, filt_b_ref, found_b_ref)
-        forward(item + 3, hid_b_ref, hid_a_ref, filt_b_ref, found_b_ref, filt_a_ref, found_a_ref)
-        return carry
-
-    lax.fori_loop(0, turns, forward_round, 0)
+    def forward_all(size):
+        def forward_round(turn, carry):
+            a = (filt_a_ref, found_a_ref)
+            b = (filt_b_ref, found_b_ref)
+            for n in range(0, 4, 2):
+                item = 4 * turn + n
+                forward(size, item, hid_a_ref, hid_b_ref, *a, *b)
+                forward(size, item + 1, hid_b_ref, hid_a_ref, *b, *a)
+            return carry
+
+        lax.fori_loop(0, turns, forward_round, 0)
+
+    most = -(-table_rows // CHUNK) * CHUNK
+    sizes = [size for size in range(most - 3 * CHUNK, most + 1, CHUNK) if size > 0]
+    for n, size in enumerate(sizes):
+        fits = packed_rows <= size
+        if n:
+            fits = fits & (packed_rows > sizes[n - 1])
+
+        @pl.when(fits)
+        def _(size=size):
+            forward_all(size)
+
     finish(4 * turns - 1, filt_b_ref, found_b_ref)
 
     message = jnp.concatenate([msg_ref[t] for t in range(tiles)], axis=1)
@@ -384,6 +422,8 @@
 
 
 def prepare(
+    lengths,
+    held,
     feat_ref,
     disp_ref,
     index_ref,
@@ -475,10 +515,14 @@
     found = dot(stack, spots)
     size = 3 * slots
     disp = found[0:size] + found[size : 2 * size] + found[2 * size : 3 * size]
-    put(
-        rows_ref.at[0],
-        found[3 * size : 3 * size + slots] * 128.0 + found[3 * size + slots : 3 * size + 2 * slots],
-    )
+    row = found[3 * size : 3 * size + slots] * 128.0 + found[3 * size + slots : 3 * size + 2 * slots]
+    put(rows_ref.at[0], row)
+    packed = row
+    edge = atoms
+    for length, used in zip(lengths[:-1], held):
+        edge += length
+        packed = packed - jnp.where(row >= float(edge), float(length) - used.astype(F32), 0.0)
+    put(rows_ref.at[8], packed)
     counts8 = dot(jnp.broadcast_to(count_row, (8, atoms)).astype(F32).astype(BF16), perm)
     counts = counts8[0:1]
     counts_ref[...] = counts8
@@ -537,7 +581,7 @@
 
 
 INPUTS = 23
-OUTPUTS = 9
+OUTPUTS = 10
 
 
 def named_faces(lists, used_ref):
@@ -554,7 +598,8 @@
     far, refs = refs[:INPUTS], refs[INPUTS:]
     table_ref, results, refs = refs[0], refs[1 : OUTPUTS + 1], refs[OUTPUTS + 1 :]
     near, made, refs = refs[:INPUTS], refs[INPUTS : INPUTS + OUTPUTS], refs[INPUTS + OUTPUTS :]
-    mine_ref, stage_ref, raw_ref, rank_ref, load_sem, save_sem, send_sem, recv_sem = refs
+    mine_ref, stage_ref, raw_ref, rank_ref, tag_ref, tags_ref, *sems = refs
+    load_sem, save_sem, send_sem, recv_sem, tag_send_sem, tag_recv_sem = sems
     loads = [
         pltpu.make_async_copy(one, two, load_sem.at[n])
         for n, (one, two) in enumerate(zip(far, near))
@@ -564,9 +609,26 @@
     found = neighbours()
     greet(found)
     feat_ref, w_ref = near[0:2]
+    used_here = near[5]
     atoms = feat_ref.shape[0]
     for load in loads[0:6]:
         load.wait()
+    used = used_here[...]
+    faces = used.shape[1]
+    tag = jnp.concatenate([used, jnp.zeros((1, LANES - faces), jnp.int32)], axis=1)
+    tag_ref[...] = jnp.broadcast_to(tag, tag_ref.shape)
+    tags = []
+    for n in range(faces):
+        tag = pltpu.make_async_remote_copy(
+            src_ref=tag_ref,
+            dst_ref=tags_ref.at[n],
+            send_sem=tag_send_sem.at[n],
+            recv_sem=tag_recv_sem.at[n],
+            device_id=found[n],
+            device_id_type=pl.DeviceIdType.MESH,
+        )
+        tag.start()
+        tags.append(tag)
     x_t = dot(feat_ref[...], w_ref[...]).T.astype(BF16)
     copies = []
     start = 0
@@ -590,7 +652,18 @@
     for load in loads[6:]:
         load.wait()
     rows_ref, order_ref, counts_ref, vals_ref, sorted_ref = made[0:5]
+    for tag in tags:
+        tag.wait()
+    held = [tags_ref[n, 0:1, face[2] : face[2] + 1] for n, face in enumerate(FACES)]
+    made[-1][...] = jnp.concatenate(
+        [jnp.broadcast_to(one, (1, LANES)) for one in held]
+        + [jnp.zeros((8 - faces, LANES), jnp.int32)],
+        axis=0,
+    )
+    lengths = [near[2 + face[0]].shape[1] for face in FACES]
     prepare(
+        lengths,
+        held,
         feat_ref,
         *near[6:12],
         rows_ref,
@@ -601,7 +674,7 @@
         raw_ref,
         rank_ref,
     )
-    ready_weights(*near[12:], *made[5:])
+    ready_weights(*near[12:], *made[5:9])
     for n, (one, two) in enumerate(zip(made, results)):
         save = pltpu.make_async_copy(one, two, save_sem.at[n + 1])
         save.start()
@@ -742,7 +815,7 @@
     hidden = w_e1.shape[1]
     anywhere = pl.BlockSpec(memory_space=pl.ANY)
     results = (
-        jax.ShapeDtypeStruct((8, steps + 1, UNROLL, LANES), F32),
+        jax.ShapeDtypeStruct((9, steps + 1, UNROLL, LANES), F32),
         jax.ShapeDtypeStruct((8, atom_rows), F32),
         jax.ShapeDtypeStruct((8, atom_rows), F32),
         jax.ShapeDtypeStruct((16, atom_rows), F32),
@@ -751,6 +824,7 @@
         jax.ShapeDtypeStruct((2, hidden, width), BF16),
         jax.ShapeDtypeStruct((2, width, hidden), BF16),
         jax.ShapeDtypeStruct((width, width), F32),
+        jax.ShapeDtypeStruct((8, LANES), jnp.int32),
     )
     table_t, rows, order, counts, vals, sorted_t, *weights = pl.pallas_call(
         send_kernel,
@@ -763,8 +837,12 @@
             pltpu.VMEM((width, ghost_rows), BF16),
             pltpu.VMEM((4, lines, LANES, LANES), F32),
             pltpu.VMEM((atom_rows, LANES), F32),
+            pltpu.VMEM((8, LANES), jnp.int32),
+            pltpu.VMEM((6, 8, LANES), jnp.int32),
             pltpu.SemaphoreType.DMA((len(inputs),)),
             pltpu.SemaphoreType.DMA((1 + len(results),)),
+            pltpu.SemaphoreType.DMA((6,)),
+            pltpu.SemaphoreType.DMA((6,)),
             pltpu.SemaphoreType.DMA((6,)),
             pltpu.SemaphoreType.DMA((6,)),
         ],
@@ -774,13 +852,13 @@
     )(*inputs)
     span = UNROLL * LANES
     energy, own_force, spread = pl.pallas_call(
-        pair_kernel,
+        functools.partial(pair_kernel, [one.shape[1] for one in lists for _ in range(2)]),
         out_shape=(
             jax.ShapeDtypeStruct((atom_rows,), F32),
             jax.ShapeDtypeStruct((8, atom_rows), F32),
             jax.ShapeDtypeStruct((groups, 8, 128), F32),
         ),
-        in_specs=[vmem] * 10,
+        in_specs=[vmem] * 10 + [pl.BlockSpec(memory_space=pltpu.SMEM)],
         out_specs=(vmem, vmem, vmem),
         scratch_shapes=[
             pltpu.VMEM((tiles, width, LANES), F32),
@@ -801,6 +879,7 @@
             pltpu.VMEM((8, span), F32),
             pltpu.VMEM((8, span), F32),
             pltpu.VMEM((3 * GROUP_ROWS, 128), F32),
+            pltpu.VMEM((width, -(-table_rows // CHUNK) * CHUNK + LANES), BF16),
         ],
         compiler_params=pltpu.CompilerParams(vmem_limit_bytes=58 * 1024 * 1024),
         cost_estimate=pl.CostEstimate(

time: 61 us -> 57.9 us (0.949)
  Pallas kernels: 58.6 us -> 55.4 us
    pallas_call x1, Pallas kernels: 36.2 us -> 32.4 us  [body(): pl.pallas_call(functools.partial(pair_kernel, [one.shape[1] for one in li...]
where the time goes in v3:
time: 57.9 us; the launch traced here: 57.4 us
  Pallas kernels  55.4 us (96%)
  local copies, waits for them, and re-layouts  1.3 us (2%)
  between operations  0.65 us (1%)
    pallas_call x1, Pallas kernels, body(): pl.pallas_call(functools.partial(pair_kernel, [one.shape[1] for one in li...  32.4 us
    pallas_call x1, Pallas kernels, body(): pl.pallas_call(send_kernel, out_shape=(jax.ShapeDtypeStruct((width, table...  13.6 us
    pallas_call x1, Pallas kernels, body(): pl.pallas_call(return_kernel, out_shape=jax.ShapeDtypeStruct((3, atom_row...  9.35 us
    unnamed x1, local copies, waits for them, and re-layouts  1.3 us

profile of v3, /device:TPU:0, one launch (start us, length us, event | category | flops | bytes accessed | tf_op | source)
XLA Modules:
  0.0 57.4 jit_solution(2807714896917078101)
XLA Ops:
  0.6 13.6 %shard_map.230 = (bf16[128,2688]{1,0:T(8,128)(2,1)}, f32[9,61,4,128]{3,2,1,0:T(4,128)}, f32[8,640]{1,0:T(8,128)}, f32[8,640]{1,0:T(8,128)}, f32[16,640]{1,0:T(8,...) custom-call(bf16[640,128]{1,0:T(8,128)(2,1)} %refs_0_.1, ...), custom_call_target="tpu_custom_call" | custom-call | tf_op jit(solution)/shard_map/pallas_call | solution.py:829
  14.3 32.4 %shard_map.231 = (f32[640]{0:T(1024)}, f32[8,640]{1,0:T(8,128)}, f32[21,8,128]{2,1,0:T(8,128)}) custom-call(f32[9,61,4,128]{3,2,1,0:T(4,128)} %get-tuple-element.16.rows_ref, f32[8,640]{1,0:T(8,128)} %get-tuple-element.17.order_ref, f32[8,640]{1,0:T(8,128)} %get-tuple-element.18.counts_ref, f32[16,640]{1,0:T(8,128)} %get-tuple-element.19.vals_ref, ...), custom_call_target="tpu_custom_call" | custom-call | flops 30000001024 | bytes 4000000 | tf_op jit(solution)/shard_map/pallas_call | solution.py:854
  46.7 9.3 %shard_map.232 = f32[3,640]{1,0:T(4,128)} custom-call(f32[8,640]{1,0:T(8,128)} %get-tuple-element.28.own_ref, f32[21,8,128]{2,1,0:T(8,128)} %get-tuple-element.29.spread_ref, f32[8,640]{1,0:T(8,128)} %get-tuple-element.17.order_ref, s32[2,640]{1,0:T(2,128)} %bitcast.7, s32[2,256]{1,0:T(2,128)} %bitcast.10, s32[2,128]{1,0:T(2,128)} %bitcast.12, s32[1,6]{1,0:T(1,128)} %used_ref.1), custom_call_target="tpu_custom_call" | custom-call | tf_op jit(solution)/shard_map/pallas_call | solution.py:899
  56.1 1.3 %copy.26 = f32[3,640]{1,0:T(4,128)} copy(f32[3,640]{1,0:T(4,128)} %shard_map.232) | data formatting | bytes 15360

commit v4 on v3

--- a/solution.py
+++ b/solution.py
@@ -67,6 +67,24 @@
 
 def flip(weight):
     return weight.astype(F32).T.astype(BF16)
+
+
+def packed_height(length):
+    return -(-3 * (length // LANES) // 8) * 8
+
+
+def unpacked(ref, at, length):
+    count = length // LANES
+    return jnp.concatenate(
+        [
+            jnp.concatenate(
+                [ref[at + c * count + h : at + c * count + h + 1] for h in range(count)], axis=1
+            )
+            for c in range(3)
+        ]
+        + [jnp.zeros((5, length), F32)],
+        axis=0,
+    )
 
 
 def pair_kernel(
@@ -83,7 +101,6 @@
     column_ref,
     held_ref,
     energy_ref,
-    own_ref,
     spread_ref,
     msg_ref,
     gm_ref,
@@ -334,11 +351,19 @@
 
     lax.fori_loop(0, rounds + 2, backward_round, 0)
 
+    spread_ref[...] = jnp.zeros_like(spread_ref)
+    group = tiles
+    at = 0
+    for length in [atoms] + list(lengths):
+        count = length // LANES
+        first = 0 if at == 0 else group
+        for c in range(3):
+            rows = total_ref[c * GROUP_ROWS + first : c * GROUP_ROWS + first + count]
+            spread_ref[at + c * count : at + (c + 1) * count] = rows
+        group = group + count if at else group
+        at += packed_height(length)
     for tile in range(tiles):
-        own_ref[:, tile * LANES : (tile + 1) * LANES] = own3_ref[tile]
-    spread_ref[...] = jnp.zeros_like(spread_ref)
-    for c in range(3):
-        spread_ref[:, c, :] = total_ref[c * GROUP_ROWS : c * GROUP_ROWS + spread_ref.shape[0]]
+        spread_ref[at + 8 * tile : at + 8 * tile + 8] = own3_ref[tile]
 
 
 def neighbours():
@@ -684,7 +709,6 @@
 
 
 def return_kernel(
-    own_ref,
     spread_ref,
     order_ref,
     ex_ref,
@@ -692,7 +716,6 @@
     ez_ref,
     used_ref,
     force_ref,
-    own_here,
     order_here,
     ex_here,
     ey_here,
@@ -705,10 +728,8 @@
     recv_sem,
 ):
     atoms = force_ref.shape[1]
-    group = atoms // 128
     pairs = (
-        (spread_ref.at[pl.ds(0, group)], mine_ref),
-        (own_ref, own_here),
+        (spread_ref, mine_ref),
         (order_ref, order_here),
         (ex_ref, ex_here),
         (ey_ref, ey_here),
@@ -723,12 +744,15 @@
     lists = (ex_here, ey_here, ez_here)
     found = neighbours()
     greet(found)
+    base = packed_height(atoms)
+    places = []
     copies = []
     start = 0
     for n, (dim, _, _, to) in enumerate(FACES):
-        length = lists[dim].shape[1] // 128
+        places.append((start, lists[dim].shape[1]))
+        length = packed_height(lists[dim].shape[1])
         copy = pltpu.make_async_remote_copy(
-            src_ref=spread_ref.at[pl.ds(group + start, length)],
+            src_ref=spread_ref.at[pl.ds(base + start, length)],
             dst_ref=land_ref.at[pl.ds(start, length)],
             send_sem=send_sem.at[n],
             recv_sem=recv_sem.at[n],
@@ -743,12 +767,14 @@
     picks = jnp.concatenate(
         [one_hot(names, atoms) for names in named_faces(lists, used_here)], axis=1
     )
-    total = jnp.concatenate([mine_ref[h] for h in range(group)], axis=1)
-    part = dot(split2(own_here[...]), one_hot(order_here[0:1], atoms))
+    total = unpacked(mine_ref, 0, atoms)
+    own = base + start
+    own = [mine_ref[own + 8 * t : own + 8 * t + 8] for t in range(atoms // LANES)]
+    part = dot(split2(jnp.concatenate(own, axis=1)), one_hot(order_here[0:1], atoms))
     total = total + part[0:8] + part[8:16]
     for copy in copies:
         copy.wait()
-    values = jnp.concatenate([land_ref[h] for h in range(start)], axis=1)
+    values = jnp.concatenate([unpacked(land_ref, *place) for place in places], axis=1)
     part = dot_nt(split2(values), picks)
     total = total + part[0:8] + part[8:16]
     force_ref[...] = total[0:3]
@@ -787,7 +813,8 @@
     table_rows = atom_rows + ghost_rows
     tiles = atom_rows // LANES
     steps = slot_count // UNROLL * tiles
-    groups = table_rows // 128
+    ghost_height = sum(2 * packed_height(one.shape[1]) for one in lists)
+    packed = packed_height(atom_rows) + ghost_height + 8 * tiles
     lines = math.lcm(slot_count, LANES) // LANES
     inputs = (
         features,
@@ -851,15 +878,14 @@
         ),
     )(*inputs)
     span = UNROLL * LANES
-    energy, own_force, spread = pl.pallas_call(
+    energy, spread = pl.pallas_call(
         functools.partial(pair_kernel, [one.shape[1] for one in lists for _ in range(2)]),
         out_shape=(
             jax.ShapeDtypeStruct((atom_rows,), F32),
-            jax.ShapeDtypeStruct((8, atom_rows), F32),
-            jax.ShapeDtypeStruct((groups, 8, 128), F32),
+            jax.ShapeDtypeStruct((packed, LANES), F32),
         ),
         in_specs=[vmem] * 10 + [pl.BlockSpec(memory_space=pltpu.SMEM)],
-        out_specs=(vmem, vmem, vmem),
+        out_specs=(vmem, vmem),
         scratch_shapes=[
             pltpu.VMEM((tiles, width, LANES), F32),
             pltpu.VMEM((tiles, width, LANES), F32),
@@ -894,8 +920,8 @@
         table_t,
         *weights,
     )
-    last = (own_force, spread, order, *lists, face_counts)
-    copied = (own_force, order, *lists, face_counts)
+    last = (spread, order, *lists, face_counts)
+    copied = (order, *lists, face_counts)
     forces = pl.pallas_call(
         return_kernel,
         out_shape=jax.ShapeDtypeStruct((3, atom_rows), F32),
@@ -903,14 +929,14 @@
         out_specs=vmem,
         scratch_shapes=[pltpu.VMEM(one.shape, one.dtype) for one in copied]
         + [
-            pltpu.VMEM((tiles, 8, LANES), F32),
-            pltpu.VMEM((ghost_rows // 128, 8, 128), F32),
+            pltpu.VMEM((packed, LANES), F32),
+            pltpu.VMEM((ghost_height, LANES), F32),
             pltpu.SemaphoreType.DMA((len(last),)),
             pltpu.SemaphoreType.DMA((6,)),
             pltpu.SemaphoreType.DMA((6,)),
         ],
         compiler_params=pltpu.CompilerParams(
-            collective_id=1, has_side_effects=True, vmem_limit_bytes=58 * 1024 * 1024
+            collective_id=1, has_side_effects=True, vmem_limit_bytes=20 * 1024 * 1024
         ),
     )(*last)
     return (energy, forces)

time: 57.9 us -> 56.8 us (0.981)
  Pallas kernels: 55.4 us -> 54.4 us
    pallas_call x1, Pallas kernels: 9.35 us -> 8.39 us  [body(): pl.pallas_call(return_kernel, out_shape=jax.ShapeDtypeStruct((3, atom_row...]
    unnamed x1 -> x13, local copies, waits for them, and re-layouts: 1.3 us -> 1.45 us
where the time goes in v4:
time: 56.8 us; the launch traced here: 56.6 us
  Pallas kernels  54.4 us (96%)
  local copies, waits for them, and re-layouts  1.45 us (3%)
  between operations  0.73 us (1%)
    pallas_call x1, Pallas kernels, body(): pl.pallas_call(functools.partial(pair_kernel, [one.shape[1] for one in li...  32.3 us
    pallas_call x1, Pallas kernels, body(): pl.pallas_call(send_kernel, out_shape=(jax.ShapeDtypeStruct((width, table...  13.6 us
    pallas_call x1, Pallas kernels, body(): pl.pallas_call(return_kernel, out_shape=jax.ShapeDtypeStruct((3, atom_row...  8.39 us
    unnamed x13, local copies, waits for them, and re-layouts  1.45 us

profile of v4, /device:TPU:0, one launch (start us, length us, event | category | flops | bytes accessed | tf_op | source)
XLA Modules:
  0.0 56.6 jit_solution(3413567285844992719)
XLA Ops:
  0.6 13.6 %shard_map.230 = (bf16[128,2688]{1,0:T(8,128)(2,1)}, f32[9,61,4,128]{3,2,1,0:T(4,128)}, f32[8,640]{1,0:T(8,128)}, f32[8,640]{1,0:T(8,128)}, f32[16,640]{1,0:T(8,...) custom-call(bf16[640,128]{1,0:T(8,128)(2,1)} %refs_0_.1, ...), custom_call_target="tpu_custom_call" | custom-call | tf_op jit(solution)/shard_map/pallas_call | solution.py:856
  14.3 0.0 copy-start.1
  14.3 0.0 copy-start.2
  14.3 0.0 copy-start.3
  14.3 0.0 copy-start.4
  14.3 0.0 copy-start.5
  14.4 32.3 %shard_map.231 = (f32[640]{0:T(1024)}, f32[120,128]{1,0:T(8,128)}) custom-call(f32[9,61,4,128]{3,2,1,0:T(4,128)} %get-tuple-element.15.rows_ref, f32[8,640]{1,0:T(8,128)} %get-tuple-element.16.order_ref, f32[8,640]{1,0:T(8,128)} %get-tuple-element.17.counts_ref, f32[16,640]{1,0:T(8,128)} %get-tuple-element.18.vals_ref, ...), custom_call_target="tpu_custom_call" | custom-call | flops 30000001024 | bytes 4000000 | tf_op jit(solution)/shard_map/pallas_call | solution.py:881
  46.7 0.0 copy-done.1
  46.7 0.0 copy-done.2
  46.7 0.0 copy-done.3
  46.7 0.0 copy-done.4
  46.7 0.0 copy-done.5
  46.7 0.0 copy-start
  46.7 0.8 %copy-done = f32[120,128]{1,0:T(8,128)S(1)} copy-done((f32[120,128]{1,0:T(8,128)S(1)}, f32[120,128]{1,0:T(8,128)}, u32[]{:S(2)}) %copy-start) | copy-done | bytes 61464
  47.6 8.4 %shard_map.232 = f32[3,640]{1,0:T(4,128)S(1)} custom-call(f32[120,128]{1,0:T(8,128)S(1)} %copy-done, f32[8,640]{1,0:T(8,128)S(1)} %copy-done.2, s32[2,640]{1,0:T(2,128)S(1)} %bitcast.6, s32[2,256]{1,0:T(2,128)S(1)} %bitcast.8, s32[2,128]{1,0:T(2,128)S(1)} %bitcast.10, s32[1,6]{1,0:T(1,128)S(1)} %copy-done.5), custom_call_target="tpu_custom_call" | custom-call | tf_op jit(solution)/shard_map/pallas_call | solution.py:925
  56.0 0.6 %copy.26 = f32[3,640]{1,0:T(4,128)} copy(f32[3,640]{1,0:T(4,128)S(1)} %shard_map.232) | data formatting | bytes 15360
Async XLA Ops:
  14.3 32.4 %copy-start.1 = (s32[1,2,640]{2,1,0:T(2,128)S(1)}, s32[1,2,640]{2,1,0:T(2,128)}, u32[]{:S(2)}) copy-start(s32[1,2,640]{2,1,0:T(2,128)} %param.28) | copy-start | bytes 15364
  14.3 32.4 %copy-start.2 = (f32[8,640]{1,0:T(8,128)S(1)}, f32[8,640]{1,0:T(8,128)}, u32[]{:S(2)}) copy-start(f32[8,640]{1,0:T(8,128)} %get-tuple-element.16.order_ref) | copy-start | bytes 61444
  14.3 32.4 %copy-start.3 = (s32[1,2,256]{2,1,0:T(2,128)S(1)}, s32[1,2,256]{2,1,0:T(2,128)}, u32[]{:S(2)}) copy-start(s32[1,2,256]{2,1,0:T(2,128)} %param.29) | copy-start | bytes 6148
  14.3 32.4 %copy-start.4 = (s32[1,2,128]{2,1,0:T(2,128)S(1)}, s32[1,2,128]{2,1,0:T(2,128)}, u32[]{:S(2)}) copy-start(s32[1,2,128]{2,1,0:T(2,128)} %param.30) | copy-start | bytes 3076
  14.3 32.4 %copy-start.5 = (s32[1,6]{1,0:T(1,128)S(1)}, s32[1,6]{1,0:T(1,128)}, u32[]{:S(2)}) copy-start(s32[1,6]{1,0:T(1,128)} %used_ref.1) | copy-start | bytes 76
  46.7 0.8 %copy-start = (f32[120,128]{1,0:T(8,128)S(1)}, f32[120,128]{1,0:T(8,128)}, u32[]{:S(2)}) copy-start(f32[120,128]{1,0:T(8,128)} %get-tuple-element.27.spread_ref) | copy-start | bytes 184324

commit v5 on v4

--- a/solution.py
+++ b/solution.py
@@ -215,15 +215,15 @@
         msg_ref[tile] = part
 
     def forward(size, item, hid_ref, next_ref, filt_ref, found_ref, last_filt_ref, last_found_ref):
-        filt = dot(w2t, hid_ref[...]) + b_f2
         slope, pre = radial_dot(place(item + 1)[1])
         slope_ref[item + BEHIND + 1] = slope
         picked = one_hot(lane_row(rows_ref.at[8], place(item)[1]), size)
         found = dot(packed_ref[:, 0:size], picked)
+        filt = dot(w2t, hid_ref[...]) + b_f2
+        finish(item - 1, last_filt_ref, last_found_ref)
         sig, hidden = activate(pre)
         sig_ref[item + BEHIND + 1] = sig
         next_ref[...] = hidden
-        finish(item - 1, last_filt_ref, last_found_ref)
         filt_ref[...] = filt
         found_ref[...] = found
         xj_ref[item + BEHIND] = found.astype(BF16)

time: 56.8 us -> 56.8 us (level)
    pallas_call x1, Pallas kernels: 32.3 us -> 34 us  [body(): pl.pallas_call(functools.partial(pair_kernel, [one.shape[1] for one in li...]
    pallas_call x1, Pallas kernels: 8.39 us -> 6.73 us  [body(): pl.pallas_call(return_kernel, out_shape=jax.ShapeDtypeStruct((3, atom_row...]
where the time goes in v5:
time: 56.8 us; the launch traced here: 56.6 us
  Pallas kernels  54.4 us (96%)
  local copies, waits for them, and re-layouts  1.45 us (3%)
  between operations  0.73 us (1%)
    pallas_call x1, Pallas kernels, body(): pl.pallas_call(functools.partial(pair_kernel, [one.shape[1] for one in li...  34 us
    pallas_call x1, Pallas kernels, body(): pl.pallas_call(send_kernel, out_shape=(jax.ShapeDtypeStruct((width, table...  13.6 us
    pallas_call x1, Pallas kernels, body(): pl.pallas_call(return_kernel, out_shape=jax.ShapeDtypeStruct((3, atom_row...  6.73 us
    unnamed x13, local copies, waits for them, and re-layouts  1.45 us

profile of v5, /device:TPU:0, one launch (start us, length us, event | category | flops | bytes accessed | tf_op | source)
XLA Modules:
  0.0 56.6 jit_solution(9194646508999819809)
XLA Ops:
  0.6 13.6 %shard_map.230 = (bf16[128,2688]{1,0:T(8,128)(2,1)}, f32[9,61,4,128]{3,2,1,0:T(4,128)}, f32[8,640]{1,0:T(8,128)}, f32[8,640]{1,0:T(8,128)}, f32[16,640]{1,0:T(8,...) custom-call(bf16[640,128]{1,0:T(8,128)(2,1)} %refs_0_.1, ...), custom_call_target="tpu_custom_call" | custom-call | tf_op jit(solution)/shard_map/pallas_call | solution.py:856
  14.3 0.0 copy-start.1
  14.3 0.0 copy-start.2
  14.3 0.0 copy-start.3
  14.3 0.0 copy-start.4
  14.3 0.0 copy-start.5
  14.4 34.0 %shard_map.231 = (f32[640]{0:T(1024)}, f32[120,128]{1,0:T(8,128)}) custom-call(f32[9,61,4,128]{3,2,1,0:T(4,128)} %get-tuple-element.15.rows_ref, f32[8,640]{1,0:T(8,128)} %get-tuple-element.16.order_ref, f32[8,640]{1,0:T(8,128)} %get-tuple-element.17.counts_ref, f32[16,640]{1,0:T(8,128)} %get-tuple-element.18.vals_ref, ...), custom_call_target="tpu_custom_call" | custom-call | flops 30000001024 | bytes 4000000 | tf_op jit(solution)/shard_map/pallas_call | solution.py:881
  48.4 0.0 copy-done.1
  48.4 0.0 copy-done.2
  48.4 0.0 copy-done.3
  48.4 0.0 copy-done.4
  48.4 0.0 copy-done.5
  48.4 0.0 copy-start
  48.4 0.8 %copy-done = f32[120,128]{1,0:T(8,128)S(1)} copy-done((f32[120,128]{1,0:T(8,128)S(1)}, f32[120,128]{1,0:T(8,128)}, u32[]{:S(2)}) %copy-start) | copy-done | bytes 61464
  49.2 6.7 %shard_map.232 = f32[3,640]{1,0:T(4,128)S(1)} custom-call(f32[120,128]{1,0:T(8,128)S(1)} %copy-done, f32[8,640]{1,0:T(8,128)S(1)} %copy-done.2, s32[2,640]{1,0:T(2,128)S(1)} %bitcast.6, s32[2,256]{1,0:T(2,128)S(1)} %bitcast.8, s32[2,128]{1,0:T(2,128)S(1)} %bitcast.10, s32[1,6]{1,0:T(1,128)S(1)} %copy-done.5), custom_call_target="tpu_custom_call" | custom-call | tf_op jit(solution)/shard_map/pallas_call | solution.py:925
  56.0 0.6 %copy.26 = f32[3,640]{1,0:T(4,128)} copy(f32[3,640]{1,0:T(4,128)S(1)} %shard_map.232) | data formatting | bytes 15360
Async XLA Ops:
  14.3 34.1 %copy-start.1 = (s32[1,2,640]{2,1,0:T(2,128)S(1)}, s32[1,2,640]{2,1,0:T(2,128)}, u32[]{:S(2)}) copy-start(s32[1,2,640]{2,1,0:T(2,128)} %param.28) | copy-start | bytes 15364
  14.3 34.1 %copy-start.2 = (f32[8,640]{1,0:T(8,128)S(1)}, f32[8,640]{1,0:T(8,128)}, u32[]{:S(2)}) copy-start(f32[8,640]{1,0:T(8,128)} %get-tuple-element.16.order_ref) | copy-start | bytes 61444
  14.3 34.1 %copy-start.3 = (s32[1,2,256]{2,1,0:T(2,128)S(1)}, s32[1,2,256]{2,1,0:T(2,128)}, u32[]{:S(2)}) copy-start(s32[1,2,256]{2,1,0:T(2,128)} %param.29) | copy-start | bytes 6148
  14.3 34.1 %copy-start.4 = (s32[1,2,128]{2,1,0:T(2,128)S(1)}, s32[1,2,128]{2,1,0:T(2,128)}, u32[]{:S(2)}) copy-start(s32[1,2,128]{2,1,0:T(2,128)} %param.30) | copy-start | bytes 3076
  14.3 34.1 %copy-start.5 = (s32[1,6]{1,0:T(1,128)S(1)}, s32[1,6]{1,0:T(1,128)}, u32[]{:S(2)}) copy-start(s32[1,6]{1,0:T(1,128)} %used_ref.1) | copy-start | bytes 76
  48.4 0.8 %copy-start = (f32[120,128]{1,0:T(8,128)S(1)}, f32[120,128]{1,0:T(8,128)}, u32[]{:S(2)}) copy-start(f32[120,128]{1,0:T(8,128)} %get-tuple-element.27.spread_ref) | copy-start | bytes 184324
